TPU v7x, 32 devices: a whole 2x2x4 slice. The times are simulated.
32 devices in a mesh: sess: 2 (over x), ctx: 16 (over z, y, core).
Axes of the slice: x: 2, y: 2, z: 4, core: 2. Of those that a mesh axis runs over, the one named last changes fastest.
Arguments:
- mamba_input: bfloat16 [2, 2048, 8192], P('sess', 'ctx'), may hold values from -6 to 6
- step_size: bfloat16 [2, 2048, 64], P('sess', 'ctx'), may hold values from 0.19921875 to 1.5
- decay_log: bfloat16 [2, 2048, 64], P('sess', 'ctx'), may hold values from -0.8 to 0
- state_write: bfloat16 [2, 2048, 512], P('sess', 'ctx'), may hold values from -0.375 to 0.375
- state_read: bfloat16 [2, 2048, 512], P('sess', 'ctx'), may hold values from -0.75 to 0.75
- skip_gain: float32 [64], replicated, may hold values from 0.1 to 1.9
- saved_states: float32 [2, 3, 64, 8192], P('sess', None, 'ctx'), may hold values from -6 to 6
- home_slot: int32 [6], replicated, may hold values from 0 to 5, each once
- turn_lengths: int32 [2, 3], P('sess'), may hold values from 1 to 1024, 2048 in all within a row
- history_lengths: int32 [2, 3], P('sess'), may hold values from 4 to 1023
- queries: bfloat16 [2, 2048, 4096], P('sess', 'ctx'), may hold values from -150 to 150
- turn_keys: bfloat16 [2, 2048, 512], P('sess', 'ctx'), may hold values from -6 to 6
- turn_values: bfloat16 [2, 2048, 512], P('sess', 'ctx'), may hold values from -6 to 6
- cache_keys: bfloat16 [2, 3, 512, 512], P('sess', None, 'ctx'), may hold values from -6 to 6
- cache_values: bfloat16 [2, 3, 512, 512], P('sess', None, 'ctx'), may hold values from -6 to 6
- sink_keys: bfloat16 [2, 3, 4, 512], P('sess'), may hold values from -12 to 12
- sink_values: bfloat16 [2, 3, 4, 512], P('sess'), may hold values from -6 to 6
Outputs:
- mixed: bfloat16 [2, 2048, 8192], P('sess', 'ctx')
- attended: bfloat16 [2, 2048, 4096], P('sess', 'ctx')
Inputs may be any that keep to these rules, and one draw needn't show every extreme that they name: `home_slot`: entry g * 3 + s names the stored state, in the group-major list of saved_states, from which session s of group g resumes.
All inputs are finite; a program needn't handle non-finite values.
Results may differ from a plain program's by a relative error of at most 0.004.
Values may be sent and summed in bfloat16 or wider, within the bound.
No kernel may reach another device: no remote copies, remote signals or barrier semaphores. Data moves between devices by JAX's collectives and lax.ppermute only.
A program may use at most 256 MiB of HBM per device.

v0:
```python
import math

import jax
import jax.numpy as jnp
from jax import lax
from jax.experimental import pallas as pl
from jax.experimental.pallas import tpu as pltpu
from jax.sharding import PartitionSpec as P

REACH = 4
SEQS = 3
SINKS = 4
H = 64
P_SIZE = 128
N = 64
G = 8
QH = 32
KVH = 4
HD = 128
WINDOW = 512
TOK = 128

HEADS_PER = H // G
PAIR = 2 * HEADS_PER
STEPS = H // PAIR
EXTRA = 16
BLOCK = 64
SPAN = WINDOW + BLOCK
COLUMNS = SPAN + 64
NEG = -1e30
TOKEN = jax.ShapeDtypeStruct((8, 128), jnp.float32)
FREE = pl.CostEstimate(flops=1024, bytes_accessed=1024, transcendentals=0)


class Scalars:
    def __init__(self, ids):
        self.place, self.group = ids[0], ids[1]
        self.one = ids[2]
        self.two = ids[2] + ids[3]
        self.ids = ids
        self.even = self.place % 2 == 0

    def history(self, session):
        return self.ids[2 + SEQS + session]

    def home(self, number):
        return self.ids[2 + 2 * SEQS + number]

    def session_at(self, position):
        return (position >= self.one).astype(jnp.int32) + (position >= self.two).astype(jnp.int32)

    def start_of(self, session):
        return jnp.where(session == 0, 0, jnp.where(session == 1, self.one, self.two))

    def last_start(self):
        first = self.place * TOK
        return jnp.maximum(self.start_of(self.session_at(first + TOK - 1)) - first, 0)


def scalars(kernel, *options):
    def body(ids, *refs):
        kernel(*options, Scalars(ids), *refs)

    return body


def params(mib=24):
    return pltpu.CompilerParams(vmem_limit_bytes=mib * 1024 * 1024)


def running_rows(dl_ref):
    k = lax.broadcasted_iota(jnp.int32, (TOK, TOK), 0)
    u = lax.broadcasted_iota(jnp.int32, (TOK, TOK), 1)
    upto = (k <= u).astype(jnp.bfloat16)
    running = jnp.dot(dl_ref[...], upto, preferred_element_type=jnp.float32)
    return dl_ref[...].astype(jnp.float32), running


def summary_kernel(
    local, meta, x_ref, dl_ref, step_ref, write_ref, _, keep_ref, send_ref, coef_s, factor_s, write_s
):
    step = pl.program_id(0)

    @pl.when(step == 0)
    def _():
        rates, running = running_rows(dl_ref)
        steps = step_ref[...].astype(jnp.float32)
        r = meta.last_start()
        lane = lax.broadcasted_iota(jnp.int32, (H, TOK), 1)
        last = running[:, TOK - 1 :]
        base = jnp.sum(jnp.where(lane < r, rates, 0.0), axis=1, keepdims=True)
        coef_s[...] = jnp.where(lane >= r, jnp.exp(last - running) * steps, 0.0)
        factor_s[...] = jnp.broadcast_to(jnp.exp(last - base), (H, TOK))
        write_s[...] = write_ref[...].astype(jnp.float32).T

    even = meta.even
    coef = coef_s[pl.ds(pl.multiple_of(step * PAIR, PAIR), PAIR), :]
    factor = factor_s[pl.ds(pl.multiple_of(step * PAIR, PAIR), PAIR), :]
    writes = write_s[pl.ds(pl.multiple_of(step * 2 * N, 2 * N), 2 * N), :]

    def summary(k):
        group = k // HEADS_PER
        loading = (writes[group * N : (group + 1) * N] * coef[k : k + 1]).astype(jnp.bfloat16)
        return jnp.dot(
            loading, x_ref[:, k * P_SIZE : (k + 1) * P_SIZE], preferred_element_type=jnp.float32
        )

    for chip in range(PAIR // (2 * local)):
        low, high = 2 * local * chip, 2 * local * chip + local
        for k in range(local):
            first, second = summary(low + k), summary(high + k)
            rows = slice(k * N, (k + 1) * N)
            keep_ref[chip, rows, :] = jnp.where(even, first, second).astype(jnp.bfloat16)
            send_ref[chip, rows, :] = jnp.where(even, second, first).astype(jnp.bfloat16)
        first, second = factor[low : low + local], factor[high : high + local]
        keep_ref[chip, local * N :, :] = factor_rows(jnp.where(even, first, second))
        send_ref[chip, local * N :, :] = factor_rows(jnp.where(even, second, first))


def factor_rows(rows):
    high = rows.astype(jnp.bfloat16).astype(jnp.float32)
    parts = [high, rows - high]
    if EXTRA > 2 * rows.shape[0]:
        parts.append(jnp.zeros((EXTRA - 2 * rows.shape[0], TOK), jnp.float32))
    return jnp.concatenate(parts, axis=0).astype(jnp.bfloat16)


def factors_of(block, local):
    block = block.astype(jnp.float32)
    return block[:local] + block[local : 2 * local]


def summaries(meta, x, rates, steps, writes, local, idle):
    chips = H // (2 * local)
    rows = local * N + EXTRA
    shape = jax.ShapeDtypeStruct((chips, rows, P_SIZE), jnp.bfloat16)
    spec = pl.BlockSpec((PAIR // (2 * local), rows, P_SIZE), lambda i, *m: (i, 0, 0))
    return pl.pallas_call(
        scalars(summary_kernel, local),
        out_shape=[shape, shape],
        grid_spec=pltpu.PrefetchScalarGridSpec(
            num_scalar_prefetch=1,
            grid=(STEPS,),
            in_specs=[
                pl.BlockSpec((TOK, PAIR * P_SIZE), lambda i, *m: (0, i)),
                pl.BlockSpec((H, TOK), lambda i, *m: (0, 0)),
                pl.BlockSpec((H, TOK), lambda i, *m: (0, 0)),
                pl.BlockSpec((TOK, G * N), lambda i, *m: (0, 0)),
                pl.BlockSpec(memory_space=pl.ANY),
            ],
            out_specs=[spec, spec],
            scratch_shapes=[
                pltpu.VMEM((H, TOK), jnp.float32),
                pltpu.VMEM((H, TOK), jnp.float32),
                pltpu.VMEM((G * N, TOK), jnp.float32),
            ],
        ),
        compiler_params=params(60),
        cost_estimate=FREE,
        name="summaries",
    )(meta, x, rates, steps, writes, idle)


def idle_spec(array):
    return pl.BlockSpec(memory_space=pl.ANY)


def whole(kernel, name, meta, arrays, shapes, idle=(), mib=24, scratch=()):
    def spec(shape):
        return pl.BlockSpec(shape, lambda i, *m: (0,) * len(shape))

    return pl.pallas_call(
        kernel,
        out_shape=[jax.ShapeDtypeStruct(s, t) for s, t in shapes],
        grid_spec=pltpu.PrefetchScalarGridSpec(
            num_scalar_prefetch=1,
            grid=(1,),
            in_specs=[spec(a.shape) for a in arrays] + [idle_spec(a) for a in idle],
            out_specs=[spec(s) for s, _ in shapes],
            scratch_shapes=scratch,
        ),
        compiler_params=params(mib),
        cost_estimate=FREE,
        name=name,
    )(meta, *arrays, *idle)


def pack_kernel(half, meta, keys_ref, values_ref, turn_keys_ref, turn_values_ref, home_ref, away_ref, band_ref):
    band_ref[0] = turn_keys_ref[...]
    band_ref[1] = turn_values_ref[...]
    rows = keys_ref.shape[1]
    upper = (meta.place >= half).astype(jnp.int32)
    for out_ref, first in ((home_ref, upper), (away_ref, 1 - upper)):
        for which, ref in enumerate((keys_ref, values_ref)):
            for s in range(2):
                for j in range(KVH):
                    place = ((which * 2 + s) * KVH + j) * rows
                    out_ref[0, place : place + rows, :] = ref[first + s, :, j * HD : (j + 1) * HD]


def turn_kernel(local, meta, stored_ref, *refs):
    out_ref = refs[-1]
    for s in range(SEQS):
        for k in range(local):
            out_ref[s, k * N : (k + 1) * N, :] = stored_ref[s, k].T


def join_kernel(meta, first_ref, second_ref, *refs):
    out_ref = refs[-1]
    count = first_ref.shape[0]
    out_ref[:count] = first_ref[...]
    out_ref[count:] = second_ref[...]


def join_two_kernel(meta, first_ref, second_ref, key_value_ref, four_ref, *refs):
    out_ref, two_ref = refs[-2:]
    count = first_ref.shape[0]
    out_ref[:count] = first_ref[...]
    out_ref[count:] = second_ref[...]
    two_ref[...] = jnp.where(meta.place // 2 % 2 == 0, key_value_ref[...], four_ref[...])


def pair_kernel(meta, key_value_ref, two_ref, four_ref, *refs):
    out_ref = refs[-1]
    key_value, two, four = key_value_ref[...], two_ref[...], four_ref[...]
    out_ref[0] = jnp.where(meta.even, key_value, two)
    out_ref[1] = jnp.where(meta.even, two, four)


def far_place(distance, bits):
    place = distance * 0
    for k in range(bits):
        place = place + ((distance // (1 << k)) % 2) * (1 << (bits - 1 - k))
    return place


def combine_kernel(local, meta, keep_ref, got_ref, *refs):
    out_ref = refs[-1]
    even = meta.even
    second = (meta.place // 2 * 2 + 1) * TOK
    closes = meta.start_of(meta.session_at(second + TOK - 1)) >= second
    width = local * N
    for chip in range(keep_ref.shape[0]):
        keep = factors_of(keep_ref[chip, width:, :], local)
        got = factors_of(got_ref[chip, width:, :], local)
        f0, f1 = jnp.where(even, keep, got), jnp.where(even, got, keep)
        out_ref[chip, width:, :] = factor_rows(jnp.where(closes, f1, f0 * f1))
        carry = jnp.where(closes, 0.0, f1)
        for k in range(local):
            rows = slice(k * N, (k + 1) * N)
            keep = keep_ref[chip, rows, :].astype(jnp.float32)
            got = got_ref[chip, rows, :].astype(jnp.float32)
            s0, s1 = jnp.where(even, keep, got), jnp.where(even, got, keep)
            out_ref[chip, rows, :] = (carry[k : k + 1] * s0 + s1).astype(jnp.bfloat16)


def recurrence_kernel(local, groups, meta, got_ref, *refs):
    stored, (out_ref, token_ref, restored_ref) = refs[:groups], refs[-3:]
    token_ref[...] = jnp.zeros_like(token_ref)
    for s in range(SEQS):
        slot = meta.home(meta.group * SEQS + s)
        source = (slot // SEQS - meta.group + groups) % groups
        kept = stored[0][slot % SEQS]
        for j in range(1, groups):
            kept = jnp.where(source == j, stored[j][slot % SEQS], kept)
        restored_ref[s] = kept
    width = local * N
    span = 2 * TOK
    state = [jnp.zeros((N, P_SIZE), jnp.float32) for _ in range(local)]
    for c in range(got_ref.shape[0]):
        first = c * span
        opening = meta.session_at(first)
        closing = meta.session_at(first + span - 1)
        opens = meta.start_of(opening) >= first
        closes = meta.start_of(closing) >= first
        factor = factors_of(got_ref[c, width:, :], local)
        for k in range(local):
            rows = slice(k * N, (k + 1) * N)
            entering = jnp.where(opens, restored_ref[opening, rows, :], state[k])
            out_ref[c, rows, :] = entering.astype(jnp.bfloat16)
            resumed = restored_ref[closing, rows, :]
            out_ref[c, width + k * N : width + (k + 1) * N, :] = resumed.astype(jnp.bfloat16)
            source = jnp.where(closes, resumed, state[k])
            state[k] = factor[k : k + 1] * source + got_ref[c, rows, :].astype(jnp.float32)


def middle_kernel(local, meta, entering_ref, keep_ref, got_ref, *refs):
    even = meta.even
    first = meta.place // 2 * 2 * TOK
    second = first + TOK
    start = meta.start_of(meta.session_at(second + TOK - 1))
    closes = (start > first) & (start < second)
    opens = start == second
    width = local * N
    own_ref, send_ref = refs[-2:]
    for chip in range(entering_ref.shape[0]):
        f0 = jnp.where(
            even,
            factors_of(keep_ref[chip, width:, :], local),
            factors_of(got_ref[chip, width:, :], local),
        )
        resumed = entering_ref[chip, width:, :].astype(jnp.float32)
        own_ref[chip, width:, :] = entering_ref[chip, width:, :]
        send_ref[chip, width:, :] = entering_ref[chip, width:, :]
        for k in range(local):
            rows = slice(k * N, (k + 1) * N)
            entering = entering_ref[chip, rows, :].astype(jnp.float32)
            s0 = jnp.where(
                even, keep_ref[chip, rows, :].astype(jnp.float32), got_ref[chip, rows, :].astype(jnp.float32)
            )
            middle = f0[k : k + 1] * jnp.where(closes, resumed[rows], entering) + s0
            middle = jnp.where(opens, resumed[rows], middle)
            own_ref[chip, rows, :] = jnp.where(even, entering, middle).astype(jnp.bfloat16)
            send_ref[chip, rows, :] = jnp.where(even, middle, entering).astype(jnp.bfloat16)


def intra_kernel(meta, skip, x_ref, dl_ref, step_ref, write_ref, read_ref, _, out_ref, token_ref, run_s, step_s):
    step = pl.program_id(0)

    @pl.when(step == 0)
    def _():
        _, running = running_rows(dl_ref)
        run_s[...] = running
        step_s[...] = step_ref[...].astype(jnp.float32)

    token_ref[...] = jnp.zeros_like(token_ref)
    heads = pl.ds(pl.multiple_of(step * PAIR, PAIR), PAIR)
    running = run_s[heads, :]
    sizes = step_s[heads, :]
    columns = running.T
    r = meta.last_start()
    t = lax.broadcasted_iota(jnp.int32, (TOK, TOK), 0)
    u = lax.broadcasted_iota(jnp.int32, (TOK, TOK), 1)
    causal = (u <= t) & ((u >= r) | (t < r))
    for group in range(2):
        part = slice(group * N, (group + 1) * N)
        products = lax.dot_general(
            read_ref[:, part], write_ref[:, part], (((1,), (1,)), ((), ())),
            preferred_element_type=jnp.float32,
        )
        products = jnp.where(causal, products, 0.0)
        for k in range(group * HEADS_PER, (group + 1) * HEADS_PER):
            difference = columns[:, k : k + 1] - running[k : k + 1]
            decay = jnp.exp(jnp.minimum(difference, 0.0))
            mixing = (products * decay * sizes[k : k + 1]).astype(jnp.bfloat16)
            place = slice(k * P_SIZE, (k + 1) * P_SIZE)
            x = x_ref[:, place]
            mixed = jnp.dot(mixing, x, preferred_element_type=jnp.float32)
            out_ref[:, place] = mixed + skip[step * PAIR + k] * x.astype(jnp.float32)


def intra(meta, skip, x, rates, steps, writes, reads, idle):
    return pl.pallas_call(
        scalars(intra_kernel),
        out_shape=[jax.ShapeDtypeStruct((TOK, H * P_SIZE), jnp.float32), TOKEN],
        grid_spec=pltpu.PrefetchScalarGridSpec(
            num_scalar_prefetch=2,
            grid=(STEPS,),
            in_specs=[
                pl.BlockSpec((TOK, PAIR * P_SIZE), lambda i, *m: (0, i)),
                pl.BlockSpec((H, TOK), lambda i, *m: (0, 0)),
                pl.BlockSpec((H, TOK), lambda i, *m: (0, 0)),
                pl.BlockSpec((TOK, 2 * N), lambda i, *m: (0, i)),
                pl.BlockSpec((TOK, 2 * N), lambda i, *m: (0, i)),
                pl.BlockSpec(memory_space=pl.ANY),
            ],
            out_specs=[
                pl.BlockSpec((TOK, PAIR * P_SIZE), lambda i, *m: (0, i)),
                pl.BlockSpec(TOKEN.shape, lambda i, *m: (0, 0)),
            ],
            scratch_shapes=[
                pltpu.VMEM((H, TOK), jnp.float32),
                pltpu.VMEM((H, TOK), jnp.float32),
            ],
        ),
        compiler_params=params(),
        cost_estimate=FREE,
        name="intra",
    )(meta, skip, x, rates, steps, writes, reads, idle)


def finish_kernel(
    local, meta, part_ref, dl_ref, step_ref, read_ref, own_ref, other_ref, out_ref, factor_s
):
    step = pl.program_id(0)
    even = meta.even
    r = meta.last_start()

    @pl.when(step == 0)
    def _():
        rates, running = running_rows(dl_ref)
        lane = lax.broadcasted_iota(jnp.int32, (H, TOK), 1)
        base = jnp.sum(jnp.where(lane < r, rates, 0.0), axis=1, keepdims=True)
        factor_s[...] = jnp.exp(jnp.minimum(running - jnp.where(lane >= r, base, 0.0), 0.0))

    factor = factor_s[pl.ds(pl.multiple_of(step * PAIR, PAIR), PAIR), :].T
    token = lax.broadcasted_iota(jnp.int32, (TOK, N), 0)
    resumed = (token >= r) & (r > 0)
    for group in range(2):
        reads = read_ref[:, group * N : (group + 1) * N].astype(jnp.float32)
        left = jnp.where(resumed, 0.0, reads)
        right = jnp.where(resumed, reads, 0.0)
        reads = jnp.concatenate([left, right], axis=1).astype(jnp.bfloat16)
        for k in range(group * HEADS_PER, (group + 1) * HEADS_PER):
            chip, half = k // (2 * local), k // local % 2
            rows = slice((k % local) * N, (k % local + 1) * N)
            own = even if half == 0 else jnp.logical_not(even)
            later = slice(rows.start + local * N, rows.stop + local * N)
            states = jnp.concatenate(
                [
                    jnp.where(own, own_ref[chip, rows, :], other_ref[chip, rows, :]),
                    jnp.where(own, own_ref[chip, later, :], other_ref[chip, later, :]),
                ],
                axis=0,
            )
            carried = jnp.dot(reads, states, preferred_element_type=jnp.float32)
            place = slice(k * P_SIZE, (k + 1) * P_SIZE)
            out_ref[:, place] = (part_ref[:, place] + factor[:, k : k + 1] * carried).astype(jnp.bfloat16)


def finish(meta, part, rates, steps, reads, own, other, local):
    chips = PAIR // (2 * local)
    width = 2 * local * N
    states = pl.BlockSpec((chips, width, P_SIZE), lambda i, *m: (i, 0, 0))
    return pl.pallas_call(
        scalars(finish_kernel, local),
        out_shape=jax.ShapeDtypeStruct((TOK, H * P_SIZE), jnp.bfloat16),
        grid_spec=pltpu.PrefetchScalarGridSpec(
            num_scalar_prefetch=1,
            grid=(STEPS,),
            in_specs=[
                pl.BlockSpec((TOK, PAIR * P_SIZE), lambda i, *m: (0, i)),
                pl.BlockSpec((H, TOK), lambda i, *m: (0, 0)),
                pl.BlockSpec((H, TOK), lambda i, *m: (0, 0)),
                pl.BlockSpec((TOK, 2 * N), lambda i, *m: (0, i)),
                states,
                states,
            ],
            out_specs=pl.BlockSpec((TOK, PAIR * P_SIZE), lambda i, *m: (0, i)),
            scratch_shapes=[pltpu.VMEM((H, TOK), jnp.float32)],
        ),
        compiler_params=params(),
        cost_estimate=FREE,
        name="finish",
    )(meta, part, rates, steps, reads, own, other)


def attend_kernel(
    meta, q_ref, band4, band3, band2, band1, band0, *refs,
):
    history_refs, (sk_ref, sv_ref), (out_ref, token_ref, key_s, value_s) = refs[:16], refs[16:18], refs[-4:]
    factor = 1.0 / math.sqrt(HD)
    first = meta.place * TOK
    r = meta.last_start()
    opening = meta.session_at(first)
    closing = meta.session_at(first + TOK - 1)
    bands = (band4, band3.at[0], band2, band1.at[0], band0)
    token_ref[...] = jnp.zeros_like(token_ref)

    def sinks(ref, session):
        rows = ref[session].astype(jnp.float32)
        spare = jnp.zeros((COLUMNS - SPAN - SINKS, HD), jnp.float32)
        return jnp.concatenate([rows, spare], axis=0).astype(jnp.bfloat16)

    length = (REACH + 1) * TOK

    def one_session(session, key_refs, value_refs, resuming, needed):
        start = meta.start_of(session) - first + WINDOW
        oldest = start - WINDOW + jnp.maximum(SINKS + WINDOW - meta.history(session), 0)

        @pl.when(needed & (start > 0))
        def _():
            row = lax.broadcasted_iota(jnp.int32, (length, WINDOW), 0)
            chips, share, _ = key_refs[0].shape
            index = lax.broadcasted_iota(jnp.int32, (1, WINDOW), 1)
            piece, index = index // (WINDOW // 4), index % (WINDOW // 4)
            near, row_in = index // share, index % share
            far = far_place(near, chips.bit_length() - 1)
            device = meta.place ^ (piece // 2 + piece % 2 * 2 + far * 4)
            place = device * share + row_in
            moved = (row == place + start - WINDOW).astype(jnp.bfloat16)
            part = (WINDOW // 4, HD)
            keys = jnp.concatenate([ref[...].reshape(part) for ref in key_refs], axis=0)
            values = jnp.concatenate([ref[...].reshape(part) for ref in value_refs], axis=0)
            history = jnp.dot(
                moved, jnp.concatenate([keys, values], axis=1), preferred_element_type=jnp.float32
            )
            for i, band in enumerate(bands):
                rows = slice(i * TOK, (i + 1) * TOK)
                index = lax.broadcasted_iota(jnp.int32, (TOK, HD), 0) + i * TOK
                turn = index >= start
                key_s[rows, :] = jnp.where(
                    turn, band[0].astype(jnp.float32), history[rows, :HD]
                ).astype(jnp.bfloat16)
                value_s[rows, :] = jnp.where(
                    turn, band[1].astype(jnp.float32), history[rows, HD:]
                ).astype(jnp.bfloat16)

        @pl.when(needed & (start <= 0))
        def _():
            for i, band in enumerate(bands):
                rows = slice(i * TOK, (i + 1) * TOK)
                key_s[rows, :] = band[0]
                value_s[rows, :] = band[1]

        for b in range(TOK // BLOCK):
            inside = (b * BLOCK + BLOCK > r) if resuming else (b * BLOCK < r)

            @pl.when(needed & inside)
            def _():
                rows = slice(b * BLOCK, b * BLOCK + SPAN)
                keys = jnp.concatenate([key_s[rows, :], sinks(sk_ref, session)], axis=0)
                values = jnp.concatenate([value_s[rows, :], sinks(sv_ref, session)], axis=0)
                tokens = slice(b * BLOCK, (b + 1) * BLOCK)
                queries = jnp.concatenate(
                    [q_ref[tokens, g * HD : (g + 1) * HD] for g in range(QH // KVH)], axis=0
                )
                scores = lax.dot_general(
                    queries, keys, (((1,), (1,)), ((), ())), preferred_element_type=jnp.float32
                )
                token = lax.broadcasted_iota(jnp.int32, (BLOCK, COLUMNS), 0)
                column = lax.broadcasted_iota(jnp.int32, (BLOCK, COLUMNS), 1)
                seen = (column > token) & (column <= token + WINDOW) & (column >= oldest - b * BLOCK)
                seen = (seen & (column < SPAN)) | ((column >= SPAN) & (column < SPAN + SINKS))
                bias = jnp.where(seen, 0.0, NEG)
                weights, sums = [], []
                for g in range(QH // KVH):
                    score = scores[g * BLOCK : (g + 1) * BLOCK] * factor + bias
                    weight = jnp.exp(score - jnp.max(score, axis=1, keepdims=True))
                    sums.append(jnp.sum(weight, axis=1, keepdims=True))
                    weights.append(weight.astype(jnp.bfloat16))
                mixed = jnp.dot(
                    jnp.concatenate(weights, axis=0), values, preferred_element_type=jnp.float32
                )
                for g in range(QH // KVH):
                    result = mixed[g * BLOCK : (g + 1) * BLOCK] / sums[g]
                    lanes = slice(g * HD, (g + 1) * HD)
                    if resuming:
                        index = lax.broadcasted_iota(jnp.int32, (BLOCK, HD), 0) + b * BLOCK
                        before = out_ref[tokens, lanes].astype(jnp.float32)
                        result = jnp.where(index >= r, result, before)
                    out_ref[tokens, lanes] = result.astype(jnp.bfloat16)

    one_session(opening, history_refs[0:4], history_refs[4:8], False, r > 0)
    one_session(closing, history_refs[8:12], history_refs[12:], True, r >= 0)


def attend(meta, queries, bands, pieces, half, sink_keys, sink_values, idle):
    chips = pieces[0].shape[0]
    share = WINDOW // (4 * chips)
    lanes = QH // KVH * HD

    def history_spec(which, last):
        def index(j, *m):
            known = Scalars(*m)
            session = known.session_at(known.place * TOK + (TOK - 1 if last else 0))
            session = session - (known.place >= half).astype(jnp.int32)
            return (0, (which * 2 + session) * KVH + j, 0)

        return pl.BlockSpec((chips, share, HD), index)

    def band_spec(array, number):
        if array.ndim == 3:
            return pl.BlockSpec((2, TOK, HD), lambda j, *m: (0, 0, j))
        return pl.BlockSpec((1, 2, TOK, HD), lambda j, *m: (number, 0, 0, j))

    pad = SEQS, SINKS, HD
    return pl.pallas_call(
        scalars(attend_kernel),
        out_shape=[jax.ShapeDtypeStruct((TOK, QH * HD), jnp.bfloat16), TOKEN],
        grid_spec=pltpu.PrefetchScalarGridSpec(
            num_scalar_prefetch=1,
            grid=(KVH,),
            in_specs=[pl.BlockSpec((TOK, lanes), lambda j, *m: (0, j))]
            + [band_spec(a, number) for a, number in zip(bands, (0, 1, 0, 0, 0))]
            + [history_spec(0, False)] * 4
            + [history_spec(1, False)] * 4
            + [history_spec(0, True)] * 4
            + [history_spec(1, True)] * 4
            + [pl.BlockSpec(pad, lambda j, *m: (0, 0, j))] * 2
            + [idle_spec(a) for a in idle],
            out_specs=[
                pl.BlockSpec((TOK, lanes), lambda j, *m: (0, j)),
                pl.BlockSpec(TOKEN.shape, lambda j, *m: (0, 0)),
            ],
            scratch_shapes=[
                pltpu.VMEM(((REACH + 1) * TOK, HD), jnp.bfloat16),
                pltpu.VMEM(((REACH + 1) * TOK, HD), jnp.bfloat16),
            ],
        ),
        compiler_params=params(),
        cost_estimate=FREE,
        name="attend",
    )(
        meta, queries, *bands, *pieces, *pieces, *pieces, *pieces, sink_keys, sink_values, *idle
    )


def shifted(block, axis, distance):
    devices = range(lax.axis_size(axis))
    return lax.ppermute(block, axis, [(i - distance, i) for i in devices if i - distance in devices])


def shards(
    mamba_input,
    step_size,
    decay_log,
    state_write,
    state_read,
    skip_gain,
    saved_states,
    home_slot,
    turn_lengths,
    history_lengths,
    queries,
    turn_keys,
    turn_values,
    cache_keys,
    cache_values,
    sink_keys,
    sink_values,
):
    place = lax.axis_index("ctx")
    group = lax.axis_index("sess")
    groups = lax.axis_size("sess")
    devices = lax.axis_size("ctx")
    local = saved_states.shape[2]
    width = local * N
    chips = devices // 2
    same_core = [list(range(core, devices, 2)) for core in range(2)]
    meta = jnp.concatenate(
        [jnp.stack([place, group]).astype(jnp.int32), turn_lengths[0], history_lengths[0], home_slot]
    )
    x, rates, steps = mamba_input[0], decay_log[0].T, step_size[0].T
    writes, reads = state_write[0], state_read[0]
    def apart(block, distance):
        return lax.ppermute(block, "ctx", [(i, i ^ distance) for i in range(devices)])

    def exchanged(block):
        return lax.all_to_all(block, "ctx", 0, 0, axis_index_groups=same_core, tiled=True)

    parcel = (1, 4 * KVH * cache_keys.shape[2], HD)
    band = (2, TOK, KVH * HD)
    near, away, key_value = whole(
        scalars(pack_kernel, devices // 2),
        "pack",
        meta,
        [cache_keys[0], cache_values[0], turn_keys[0], turn_values[0]],
        [(parcel, jnp.bfloat16), (parcel, jnp.bfloat16), (band, jnp.bfloat16)],
        mib=60,
    )
    distance = devices // 2
    moved = apart(away, distance)
    four = shifted(key_value, "ctx", 4)

    keep, send = summaries(meta, x, rates, steps, writes, local, away)
    got = apart(send, 1)

    def joined(array):
        return ((2 * array.shape[0], *array.shape[1:]), jnp.bfloat16)

    near, two = whole(
        scalars(join_two_kernel),
        "join_two",
        meta,
        [near, moved, key_value, four],
        [joined(near), (band, jnp.bfloat16)],
        idle=[send],
    )
    distance //= 2
    moved = apart(near, distance)

    [turned] = whole(
        scalars(turn_kernel, local),
        "turn",
        meta,
        [saved_states[0].reshape(SEQS, local, P_SIZE, N)],
        [((SEQS, width, P_SIZE), jnp.float32)],
        idle=[two],
    )
    stored = [turned]
    for j in range(1, groups):
        route = [((i + j) % groups, i) for i in range(groups)]
        stored.append(lax.ppermute(turned, "sess", route))
    after = turned
    while distance > 2:
        [near] = whole(scalars(join_kernel), "join", meta, [near, moved], [joined(near)], idle=[after])
        after = near
        distance //= 2
        moved = apart(near, distance)

    [chip] = whole(
        scalars(combine_kernel, local),
        "combine",
        meta,
        [keep, got],
        [(keep.shape, jnp.bfloat16)],
        idle=[after],
    )
    total = exchanged(chip)
    beside = moved
    across = apart(near, 1)
    two = apart(two, 2)
    part, token = intra(meta, skip_gain, x, rates, steps, writes, reads, chip)

    entering, after = whole(
        scalars(recurrence_kernel, local, groups),
        "recurrence",
        meta,
        [total, *stored],
        [((chips, 2 * width, P_SIZE), jnp.bfloat16), (TOKEN.shape, TOKEN.dtype)],
        idle=[token, beside, across, two],
        scratch=[pltpu.VMEM((SEQS, width, P_SIZE), jnp.float32)],
    )
    entering = exchanged(entering)
    [pair] = whole(
        scalars(pair_kernel), "pair", meta, [key_value, two, four], [((2, *band), jnp.bfloat16)], idle=[after]
    )
    pair = apart(pair, 1)
    pieces = [near, beside, across, apart(beside, 1)]
    bands = [four, pair, two, pair, key_value]
    attended, token = attend(
        meta, queries[0], bands, pieces, devices // 2, sink_keys[0], sink_values[0], [after]
    )
    own, other = whole(
        scalars(middle_kernel, local),
        "middle",
        meta,
        [entering, keep, got],
        [((chips, 2 * width, P_SIZE), jnp.bfloat16)] * 2,
        idle=[token],
    )
    other = apart(other, 1)
    mixed = finish(meta, part, rates, steps, reads, own, other, local)
    return mixed[None], attended[None]


def solution(mesh):
    token = P("sess", "ctx", None)
    return jax.shard_map(
        shards,
        mesh=mesh,
        in_specs=(
            token,
            token,
            token,
            token,
            token,
            P(),
            P("sess", None, "ctx", None),
            P(),
            P("sess", None),
            P("sess", None),
            token,
            token,
            token,
            P("sess", None, "ctx", None),
            P("sess", None, "ctx", None),
            P("sess", None, None, None),
            P("sess", None, None, None),
        ),
        out_specs=(token, token),
        check_vma=False,
    )
```

profile of v0, /device:TPU:0, one launch (start us, length us, event | category | flops | bytes accessed | tf_op | source)
XLA Modules:
  0.0 121.0 jit_solution(11235298337610109127)
XLA Ops:
  0.6 1.3 %concatenate.3.ids = s32[14]{0:T(128)} concatenate(s32[1]{0:T(128)} %bitcast, s32[1]{0:T(128)} %bitcast.1, s32[3]{0:T(128)} %bitcast.42, s32[3]{0:T(128)} %bitcast.43, s32[6]{0:T(128)} %param.24), dimensions={0} | concatenate | bytes 112 | tf_op jit(solution)/shard_map/concatenate | solution.py:631
  1.9 2.7 %pack.1 = (bf16[1,512,128]{2,1,0:T(8,128)(2,1)}, bf16[1,512,128]{2,1,0:T(8,128)(2,1)}, bf16[2,128,512]{2,1,0:T(8,128)(2,1)}) custom-call(s32[14]{0:T(128)} %concatenate.3.ids, bf16[3,32,512]{2,1,0:T(8,128)(2,1)} %bitcast.40, bf16[3,32,512]{2,1,0:T(8,128)(2,1)} %bitcast.41, bf16[128,512]{1,0:T(8,128)(2,1)} %bitcast.38, bf16[128,512]{1,0:T(8,128)(2,1)} %bitcast.39), custom_call_target="tpu_custom_call" | custom-call | flops 1024 | bytes 1024 | tf_op jit(solution)/shard_map/pack/pallas_call | solution.py:172
  4.6 5.2 %summaries.1 = (bf16[8,272,128]{2,1,0:T(8,128)(2,1)}, bf16[8,272,128]{2,1,0:T(8,128)(2,1)}) custom-call(s32[14]{0:T(128)} %concatenate.3.ids, bf16[128,8192]{1,0:T(8,128)(2,1)} %bitcast.22, bf16[64,128]{1,0:T(8,128)(2,1)} %bitcast.29, bf16[64,128]{1,0:T(8,128)(2,1)} %bitcast.32, bf16[128,512]{1,0:T(8,128)(2,1)} %bitcast.27, ...), custom_call_target="tpu_custom_call" | custom-call | flops 1024 | bytes 1024 | tf_op jit(solution)/shard_map/summaries/pallas_call | solution.py:138
  9.8 0.5 collective-permute-start
  10.3 4.5 %collective-permute-start.2 = (bf16[2,128,512]{2,1,0:T(8,128)(2,1)S(1)}, bf16[2,128,512]{2,1,0:T(8,128)(2,1)S(1)}, u32[]{:S(2)}, u32[]{:S(2)}) collective-permute-start(bf16[2,128,512]{2,1,0:T(8,128)(2,1)S(1)} %copy-done.3), channel_id=1, source_target_pairs={{0,4},{1,5},{2,6},{3,7},{4,8},{5,9},{6,10},{7,11},{8,12},{9,13},{1... | collective-permute-start | bytes 786440 | tf_op jit(solution)/shard_map/ppermute | solution.py:601
  14.8 2.6 %collective-permute-start.1 = (bf16[1,512,128]{2,1,0:T(8,128)(2,1)S(1)}, bf16[1,512,128]{2,1,0:T(8,128)(2,1)S(1)}, u32[]{:S(2)}, u32[]{:S(2)}) collective-permute-start(bf16[1,512,128]{2,1,0:T(8,128)(2,1)S(1)} %copy-done.36), channel_id=1, source_target_pairs={{0,8},{1,9},{2,10},{3,11},{4,12},{5,13},{6,14},{7,15},{8,0},{9,1},... | collective-permute-start | bytes 393224 | tf_op jit(solution)/shard_map/ppermute | solution.py:637
  17.5 6.7 %collective-permute-done.1.refs_1_ = bf16[1,512,128]{2,1,0:T(8,128)(2,1)S(1)} collective-permute-done((bf16[1,512,128]{2,1,0:T(8,128)(2,1)S(1)}, bf16[1,512,128]{2,1,0:T(8,128)(2,1)S(1)}, u32[]{:S(2)}, u32[]{:S(2)}) %collective-permute-start.1) | collective-permute-done | bytes 131104 | tf_op jit(solution)/shard_map/ppermute | solution.py:637
  24.2 0.0 collective-permute-done.2.refs_3_.refs_2_.refs_1_
  24.2 0.0 copy-start.10
  24.2 1.0 copy-done.10
  25.3 0.6 join_two.1
  25.9 0.0 copy-start.16
  25.9 4.0 %collective-permute-start.3 = (bf16[2,512,128]{2,1,0:T(8,128)(2,1)S(1)}, bf16[2,512,128]{2,1,0:T(8,128)(2,1)}, u32[]{:S(2)}, u32[]{:S(2)}) collective-permute-start(bf16[2,512,128]{2,1,0:T(8,128)(2,1)S(1)} %get-tuple-element.22.refs_0_), channel_id=1, source_target_pairs={{0,4},{1,5},{2,6},{3,7},{4,0},{5,1},{6,2},{7,3},{8,12},{9,13},{10,... | collective-permute-start | bytes 786440 | tf_op jit(solution)/shard_map/ppermute | solution.py:637
  29.9 0.4 reshape_squeeze.3.refs_0_
  30.4 0.8 turn.1.refs_2_.refs_1_
  31.2 0.0 copy-start.11
  31.2 5.0 %collective-permute-done.3.refs_1_ = bf16[2,512,128]{2,1,0:T(8,128)(2,1)} collective-permute-done((bf16[2,512,128]{2,1,0:T(8,128)(2,1)S(1)}, bf16[2,512,128]{2,1,0:T(8,128)(2,1)}, u32[]{:S(2)}, u32[]{:S(2)}) %collective-permute-start.3) | collective-permute-done | bytes 262176 | tf_op jit(solution)/shard_map/ppermute | solution.py:637
  36.2 0.9 copy-done.17
  37.2 1.5 %join.1.refs_2_.refs_6_.refs_10_.refs_14_.refs_18_ = bf16[4,512,128]{2,1,0:T(8,128)(2,1)S(1)} custom-call(s32[14]{0:T(128)S(1)} %copy-done.22, bf16[2,512,128]{2,1,0:T(8,128)(2,1)S(1)} %copy-done.17, bf16[2,512,128]{2,1,0:T(8,128)(2,1)} %collective-permute-done.3.refs_1_, f32[3,256,128]{2,1,0:T(8,128)S(1)} %turn.1.refs_2_.refs_1_), custom_call_target="tpu_custom_call" | custom-call | flops 1024 | bytes 1024 | tf_op jit(solution)/shard_map/join/pallas_call | solution.py:172
  38.8 1.6 %combine.1.refs_6_ = bf16[8,272,128]{2,1,0:T(8,128)(2,1)} custom-call(s32[14]{0:T(128)S(1)} %copy-done.22, bf16[8,272,128]{2,1,0:T(8,128)(2,1)S(1)} %copy-done.4, bf16[8,272,128]{2,1,0:T(8,128)(2,1)S(1)} %collective-permute-done.refs_1_.refs_2_, bf16[4,512,128]{2,1,0:T(8,128)(2,1)S(1)} %join.1.refs_2_.refs_6_.refs_10_.refs_14_.refs_18_), custom_call_target="tpu_custom_call" | custom-call | flops 1024 | bytes 1024 | tf_op jit(solution)/shard_map/combine/pallas_call | solution.py:172
  40.4 6.8 %all-to-all-start = ((bf16[8,272,128]{2,1,0:T(8,128)(2,1)}), bf16[8,272,128]{2,1,0:T(8,128)(2,1)S(1)}, u32[]{:S(2)}, u32[]{:S(2)}) async-start(bf16[8,272,128]{2,1,0:T(8,128)(2,1)} %combine.1.refs_6_), calls=%async_computation | async-start | bytes 1114112 | tf_op jit(solution)/shard_map/all_to_all | solution.py:640
  47.2 0.0 collective-permute-start.6
  47.2 2.0 %collective-permute-start.5 = (bf16[4,512,128]{2,1,0:T(8,128)(2,1)S(1)}, bf16[4,512,128]{2,1,0:T(8,128)(2,1)S(1)}, u32[]{:S(2)}, u32[]{:S(2)}) collective-permute-start(bf16[4,512,128]{2,1,0:T(8,128)(2,1)S(1)} %join.1.refs_2_.refs_6_.refs_10_.refs_14_.refs_18_), channel_id=1, source_target_pairs={{0,2},{1,3},{2,0},{3,1},{4,6},{5,7},{6,4},{7,5},{8,10},{9,11},{10,... | collective-permute-start | bytes 1572872 | tf_op jit(solution)/shard_map/ppermute | solution.py:637
  49.2 1.5 %collective-permute-start.4 = (f32[3,256,128]{2,1,0:T(8,128)S(1)}, f32[3,256,128]{2,1,0:T(8,128)S(1)}, u32[]{:S(2)}, u32[]{:S(2)}) collective-permute-start(f32[3,256,128]{2,1,0:T(8,128)S(1)} %turn.1.refs_2_.refs_1_), channel_id=1, source_target_pairs={{16,0},{0,16},{17,1},{1,17},{18,2},{2,18},{19,3},{3,19},{20,4},{4,... | collective-permute-start | bytes 1179656 | tf_op jit(solution)/shard_map/ppermute | solution.py:684
  50.7 0.1 collective-permute-start.7
  50.8 0.0 copy-start
  50.8 1.6 %copy-done = bf16[1,128,8192]{2,1,0:T(8,128)(2,1)S(1)} copy-done((bf16[1,128,8192]{2,1,0:T(8,128)(2,1)S(1)}, bf16[1,128,8192]{2,1,0:T(8,128)(2,1)}, u32[]{:S(2)}) %copy-start) | copy-done | bytes 2097176
  52.4 0.9 copy-done.12
  53.3 4.1 %intra.1 = (f32[128,8192]{1,0:T(8,128)S(1)}, f32[8,128]{1,0:T(8,128)S(1)}) custom-call(s32[14]{0:T(128)S(1)} %copy-done.23, f32[64]{0:T(128)S(1)} %copy-done.34, bf16[128,8192]{1,0:T(8,128)(2,1)S(1)} %bitcast.23, bf16[64,128]{1,0:T(8,128)(2,1)S(1)} %bitcast.30, bf16[64,128]{1,0:T(8,128)(2,1)S(1)} %bitcast.33, bf16[128,512]{1,0:T(8,128)(2,1)S(1)} %bitcast.28, ...), custom_call_target="tpu_custom_call" | custom-call | flops 1024 | bytes 1024 | tf_op jit(solution)/shard_map/intra/pallas_call | solution.py:353
  57.4 2.0 %copy-done.1 = f32[128,8192]{1,0:T(8,128)} copy-done((f32[128,8192]{1,0:T(8,128)}, f32[128,8192]{1,0:T(8,128)S(1)}, u32[]{:S(2)}) %copy-start.1) | copy-done | bytes 4194328
  59.4 12.8 %collective-permute-done.7.refs_6_.refs_1_.refs_3_ = bf16[2,128,512]{2,1,0:T(8,128)(2,1)S(1)} collective-permute-done((bf16[2,128,512]{2,1,0:T(8,128)(2,1)}, bf16[2,128,512]{2,1,0:T(8,128)(2,1)S(1)}, u32[]{:S(2)}, u32[]{:S(2)}) %collective-permute-start.7) | collective-permute-done | bytes 262176 | tf_op jit(solution)/shard_map/ppermute | solution.py:637
  72.2 0.0 collective-permute-done.4.refs_2_
  72.2 0.7 copy-done.13
  73.0 0.0 collective-permute-done.5.refs_4_.refs_7_.refs_11_.refs_15_.refs_19_
  73.0 0.0 all-to-all-done.refs_0_
  73.0 1.0 copy-done.14
  74.0 0.8 recurrence.1
  74.8 0.0 copy-start.9
  74.8 1.0 copy-done.9
  75.8 0.6 copy-done.27
  76.4 4.4 %all-to-all-start.1 = ((bf16[8,512,128]{2,1,0:T(8,128)(2,1)}), bf16[8,512,128]{2,1,0:T(8,128)(2,1)S(1)}, u32[]{:S(2)}, u32[]{:S(2)}) async-start(bf16[8,512,128]{2,1,0:T(8,128)(2,1)} %copy-done.9), calls=%async_computation.1 | async-start | bytes 2097152 | tf_op jit(solution)/shard_map/all_to_all | solution.py:640
  80.8 0.0 collective-permute-start.9
  80.8 0.6 copy-done.24
  81.4 0.7 copy-done.28
  82.0 0.6 pair.1
  82.6 0.6 collective-permute-start.8
  83.2 0.0 collective-permute-done.9.refs_9_.refs_13_.refs_17_.refs_21_
  83.2 1.5 %collective-permute-done.8.refs_2_.refs_4_ = bf16[2,2,128,512]{3,2,1,0:T(8,128)(2,1)S(1)} collective-permute-done((bf16[2,2,128,512]{3,2,1,0:T(8,128)(2,1)S(1)}, bf16[2,2,128,512]{3,2,1,0:T(8,128)(2,1)S(1)}, u32[]{:S(2)}, u32[]{:S(2)}) %collective-permute-start.8) | collective-permute-done | bytes 524320 | tf_op jit(solution)/shard_map/ppermute | solution.py:637
  84.8 1.2 %copy-done.8 = bf16[1,128,4096]{2,1,0:T(8,128)(2,1)S(1)} copy-done((bf16[1,128,4096]{2,1,0:T(8,128)(2,1)S(1)}, bf16[1,128,4096]{2,1,0:T(8,128)(2,1)}, u32[]{:S(2)}) %copy-start.8) | copy-done | bytes 1048600
  86.0 0.6 copy-done.25
  86.6 0.7 copy-done.29
  87.3 0.7 copy-done.30
  88.0 0.7 copy-done.31
  88.7 18.0 %attend.1 = (bf16[128,4096]{1,0:T(8,128)(2,1)}, f32[8,128]{1,0:T(8,128)S(1)}) custom-call(s32[14]{0:T(128)S(1)} %copy-done.25, bf16[128,4096]{1,0:T(8,128)(2,1)S(1)} %bitcast.24, bf16[2,128,512]{2,1,0:T(8,128)(2,1)S(1)} %collective-permute-done.2.refs_3_.refs_2_.refs_1_, bf16[2,2,128,512]{3,2,1,0:T(8,128)(2,1)S(1)} %collective-permute-done.8.refs_2_.refs_4_, ...), custom_call_target="tpu_custom_call" | custom-call | flops 1024 | bytes 1024 | tf_op jit(solution)/shard_map/attend/pallas_call | solution.py:568
  106.6 0.6 copy-done.32
  107.2 1.1 copy-done.5
  108.3 1.1 copy-done.7
  109.3 0.6 copy-done.26
  109.9 0.7 copy-done.33
  110.6 1.1 middle.1
  111.7 0.1 collective-permute-start.10
  111.8 2.6 %collective-permute-done.10.refs_5_ = bf16[8,512,128]{2,1,0:T(8,128)(2,1)S(1)} collective-permute-done((bf16[8,512,128]{2,1,0:T(8,128)(2,1)S(1)}, bf16[8,512,128]{2,1,0:T(8,128)(2,1)S(1)}, u32[]{:S(2)}, u32[]{:S(2)}) %collective-permute-start.10) | collective-permute-done | bytes 1048608 | tf_op jit(solution)/shard_map/ppermute | solution.py:637
  114.5 2.2 %copy-done.2 = f32[128,8192]{1,0:T(8,128)S(1)} copy-done((f32[128,8192]{1,0:T(8,128)S(1)}, f32[128,8192]{1,0:T(8,128)}, u32[]{:S(2)}) %copy-start.2) | copy-done | bytes 4194328
  116.7 4.3 %finish.1 = bf16[128,8192]{1,0:T(8,128)(2,1)} custom-call(s32[14]{0:T(128)S(1)} %copy-done.26, f32[128,8192]{1,0:T(8,128)S(1)} %copy-done.2, bf16[64,128]{1,0:T(8,128)(2,1)S(1)} %bitcast.31, bf16[64,128]{1,0:T(8,128)(2,1)S(1)} %bitcast.34, bf16[128,512]{1,0:T(8,128)(2,1)S(1)} %bitcast.26, bf16[8,512,128]{2,1,0:T(8,128)(2,1)S(1)} %get-tuple-element.29.refs_4_, ...), custom_call_target="tpu_custom_call" | custom-call | flops 1024 | bytes 1024 | tf_op jit(solution)/shard_map/finish/pallas_call | solution.py:425
  (50 shorter events, 0.1 us)
Async XLA Ops:
  1.9 22.3 %copy-start.22 = (s32[14]{0:T(128)S(1)}, s32[14]{0:T(128)}, u32[]{:S(2)}) copy-start(s32[14]{0:T(128)} %concatenate.3.ids) | copy-start | bytes 172
  1.9 28.0 %copy-start.35 = (f32[1,3,4,8192]{3,2,1,0:T(4,128)S(1)}, f32[1,3,4,8192]{3,2,1,0:T(4,128)}, u32[]{:S(2)}) copy-start(f32[1,3,4,8192]{3,2,1,0:T(4,128)} %param.23) | copy-start | bytes 1179652
  4.6 5.7 %copy-start.3 = (bf16[2,128,512]{2,1,0:T(8,128)(2,1)S(1)}, bf16[2,128,512]{2,1,0:T(8,128)(2,1)}, u32[]{:S(2)}) copy-start(bf16[2,128,512]{2,1,0:T(8,128)(2,1)} %get-tuple-element.21.refs_2_.refs_0_.refs_5_) | copy-start | bytes 786436
  4.6 10.2 %copy-start.36 = (bf16[1,512,128]{2,1,0:T(8,128)(2,1)S(1)}, bf16[1,512,128]{2,1,0:T(8,128)(2,1)}, u32[]{:S(2)}) copy-start(bf16[1,512,128]{2,1,0:T(8,128)(2,1)} %get-tuple-element.17.refs_4_) | copy-start | bytes 393220
  4.6 19.6 %copy-start.21 = (bf16[1,512,128]{2,1,0:T(8,128)(2,1)S(1)}, bf16[1,512,128]{2,1,0:T(8,128)(2,1)}, u32[]{:S(2)}) copy-start(bf16[1,512,128]{2,1,0:T(8,128)(2,1)} %get-tuple-element.20.refs_0_) | copy-start | bytes 393220
  9.8 28.9 %collective-permute-start = (bf16[8,272,128]{2,1,0:T(8,128)(2,1)}, bf16[8,272,128]{2,1,0:T(8,128)(2,1)S(1)}, u32[]{:S(2)}, u32[]{:S(2)}) collective-permute-start(bf16[8,272,128]{2,1,0:T(8,128)(2,1)} %get-tuple-element.19.refs_4_), channel_id=1, source_target_pairs={{0,1},{1,0},{2,3},{3,2},{4,5},{5,4},{6,7},{7,6},{8,9},{9,8},{10,11... | collective-permute-start | bytes 1671176 | tf_op jit(solution)/shard_map/ppermute | solution.py:637
  10.3 13.9 %collective-permute-start.2 = (bf16[2,128,512]{2,1,0:T(8,128)(2,1)S(1)}, bf16[2,128,512]{2,1,0:T(8,128)(2,1)S(1)}, u32[]{:S(2)}, u32[]{:S(2)}) collective-permute-start(bf16[2,128,512]{2,1,0:T(8,128)(2,1)S(1)} %copy-done.3), channel_id=1, source_target_pairs={{0,4},{1,5},{2,6},{3,7},{4,8},{5,9},{6,10},{7,11},{8,12},{9,13},{1... | collective-permute-start | bytes 786440 | tf_op jit(solution)/shard_map/ppermute | solution.py:601
  14.8 9.4 %collective-permute-start.1 = (bf16[1,512,128]{2,1,0:T(8,128)(2,1)S(1)}, bf16[1,512,128]{2,1,0:T(8,128)(2,1)S(1)}, u32[]{:S(2)}, u32[]{:S(2)}) collective-permute-start(bf16[1,512,128]{2,1,0:T(8,128)(2,1)S(1)} %copy-done.36), channel_id=1, source_target_pairs={{0,8},{1,9},{2,10},{3,11},{4,12},{5,13},{6,14},{7,15},{8,0},{9,1},... | collective-permute-start | bytes 393224 | tf_op jit(solution)/shard_map/ppermute | solution.py:637
  24.2 1.1 copy-start.10
  25.9 5.3 %copy-start.15 = (bf16[2,128,512]{2,1,0:T(8,128)(2,1)}, bf16[2,128,512]{2,1,0:T(8,128)(2,1)S(1)}, u32[]{:S(2)}) copy-start(bf16[2,128,512]{2,1,0:T(8,128)(2,1)S(1)} %get-tuple-element.23.refs_1_) | copy-start | bytes 786436
  25.9 5.3 %copy-start.16 = (bf16[2,512,128]{2,1,0:T(8,128)(2,1)}, bf16[2,512,128]{2,1,0:T(8,128)(2,1)S(1)}, u32[]{:S(2)}) copy-start(bf16[2,512,128]{2,1,0:T(8,128)(2,1)S(1)} %get-tuple-element.22.refs_0_) | copy-start | bytes 786436
  25.9 12.9 %copy-start.4 = (bf16[8,272,128]{2,1,0:T(8,128)(2,1)S(1)}, bf16[8,272,128]{2,1,0:T(8,128)(2,1)}, u32[]{:S(2)}) copy-start(bf16[8,272,128]{2,1,0:T(8,128)(2,1)} %get-tuple-element.18.refs_0_.refs_1_) | copy-start | bytes 1671172
  25.9 10.3 %collective-permute-start.3 = (bf16[2,512,128]{2,1,0:T(8,128)(2,1)S(1)}, bf16[2,512,128]{2,1,0:T(8,128)(2,1)}, u32[]{:S(2)}, u32[]{:S(2)}) collective-permute-start(bf16[2,512,128]{2,1,0:T(8,128)(2,1)S(1)} %get-tuple-element.22.refs_0_), channel_id=1, source_target_pairs={{0,4},{1,5},{2,6},{3,7},{4,0},{5,1},{6,2},{7,3},{8,12},{9,13},{10,... | collective-permute-start | bytes 786440 | tf_op jit(solution)/shard_map/ppermute | solution.py:637
  31.2 19.6 %copy-start.11 = (bf16[1,128,512]{2,1,0:T(8,128)(2,1)S(1)}, bf16[1,128,512]{2,1,0:T(8,128)(2,1)}, u32[]{:S(2)}) copy-start(bf16[1,128,512]{2,1,0:T(8,128)(2,1)} %param.21) | copy-start | bytes 393220
  36.2 1.0 copy-start.17
  37.2 13.6 %copy-start.18 = (bf16[1,128,64]{1,2,0:T(8,128)(2,1)S(1)}, bf16[1,128,64]{1,2,0:T(8,128)(2,1)}, u32[]{:S(2)}) copy-start(bf16[1,128,64]{1,2,0:T(8,128)(2,1)} %param.19) | copy-start | bytes 49156
  37.2 13.6 %copy-start.19 = (bf16[1,128,64]{1,2,0:T(8,128)(2,1)S(1)}, bf16[1,128,64]{1,2,0:T(8,128)(2,1)}, u32[]{:S(2)}) copy-start(bf16[1,128,64]{1,2,0:T(8,128)(2,1)} %param.18) | copy-start | bytes 49156
  37.2 13.6 %copy-start.23 = (s32[14]{0:T(128)S(1)}, s32[14]{0:T(128)}, u32[]{:S(2)}) copy-start(s32[14]{0:T(128)} %concatenate.3.ids) | copy-start | bytes 172
  37.2 13.6 %copy-start.34 = (f32[64]{0:T(128)S(1)}, f32[64]{0:T(128)}, u32[]{:S(2)}) copy-start(f32[64]{0:T(128)} %refs_0_.1) | copy-start | bytes 772
  38.7 1.6 %copy-start.6 = (bf16[8,272,128]{2,1,0:T(8,128)(2,1)}, bf16[8,272,128]{2,1,0:T(8,128)(2,1)S(1)}, u32[]{:S(2)}) copy-start(bf16[8,272,128]{2,1,0:T(8,128)(2,1)S(1)} %collective-permute-done.refs_1_.refs_2_) | copy-start | bytes 1671172
  40.4 32.6 %all-to-all-start = ((bf16[8,272,128]{2,1,0:T(8,128)(2,1)}), bf16[8,272,128]{2,1,0:T(8,128)(2,1)S(1)}, u32[]{:S(2)}, u32[]{:S(2)}) async-start(bf16[8,272,128]{2,1,0:T(8,128)(2,1)} %combine.1.refs_6_), calls=%async_computation | async-start | bytes 1114112 | tf_op jit(solution)/shard_map/all_to_all | solution.py:640
  47.2 25.8 %collective-permute-start.6 = (bf16[4,512,128]{2,1,0:T(8,128)(2,1)S(1)}, bf16[4,512,128]{2,1,0:T(8,128)(2,1)S(1)}, u32[]{:S(2)}, u32[]{:S(2)}) collective-permute-start(bf16[4,512,128]{2,1,0:T(8,128)(2,1)S(1)} %join.1.refs_2_.refs_6_.refs_10_.refs_14_.refs_18_), channel_id=1, source_target_pairs={{0,1},{1,0},{2,3},{3,2},{4,5},{5,4},{6,7},{7,6},{8,9},{9,8},{10,11... | collective-permute-start | bytes 1572872 | tf_op jit(solution)/shard_map/ppermute | solution.py:637
  47.2 25.8 %collective-permute-start.5 = (bf16[4,512,128]{2,1,0:T(8,128)(2,1)S(1)}, bf16[4,512,128]{2,1,0:T(8,128)(2,1)S(1)}, u32[]{:S(2)}, u32[]{:S(2)}) collective-permute-start(bf16[4,512,128]{2,1,0:T(8,128)(2,1)S(1)} %join.1.refs_2_.refs_6_.refs_10_.refs_14_.refs_18_), channel_id=1, source_target_pairs={{0,2},{1,3},{2,0},{3,1},{4,6},{5,7},{6,4},{7,5},{8,10},{9,11},{10,... | collective-permute-start | bytes 1572872 | tf_op jit(solution)/shard_map/ppermute | solution.py:637
  49.2 23.0 %collective-permute-start.4 = (f32[3,256,128]{2,1,0:T(8,128)S(1)}, f32[3,256,128]{2,1,0:T(8,128)S(1)}, u32[]{:S(2)}, u32[]{:S(2)}) collective-permute-start(f32[3,256,128]{2,1,0:T(8,128)S(1)} %turn.1.refs_2_.refs_1_), channel_id=1, source_target_pairs={{16,0},{0,16},{17,1},{1,17},{18,2},{2,18},{19,3},{3,19},{20,4},{4,... | collective-permute-start | bytes 1179656 | tf_op jit(solution)/shard_map/ppermute | solution.py:684
  50.7 21.6 %collective-permute-start.7 = (bf16[2,128,512]{2,1,0:T(8,128)(2,1)}, bf16[2,128,512]{2,1,0:T(8,128)(2,1)S(1)}, u32[]{:S(2)}, u32[]{:S(2)}) collective-permute-start(bf16[2,128,512]{2,1,0:T(8,128)(2,1)} %copy-done.15), channel_id=1, source_target_pairs={{0,2},{1,3},{2,0},{3,1},{4,6},{5,7},{6,4},{7,5},{8,10},{9,11},{10,... | collective-permute-start | bytes 786440 | tf_op jit(solution)/shard_map/ppermute | solution.py:637
  50.8 1.6 %copy-start = (bf16[1,128,8192]{2,1,0:T(8,128)(2,1)S(1)}, bf16[1,128,8192]{2,1,0:T(8,128)(2,1)}, u32[]{:S(2)}) copy-start(bf16[1,128,8192]{2,1,0:T(8,128)(2,1)} %param.17) | copy-start | bytes 6291460
  52.4 0.9 copy-start.12
  57.4 2.0 %copy-start.1 = (f32[128,8192]{1,0:T(8,128)}, f32[128,8192]{1,0:T(8,128)S(1)}, u32[]{:S(2)}) copy-start(f32[128,8192]{1,0:T(8,128)S(1)} %get-tuple-element.24.refs_0_) | copy-start | bytes 12582916
  72.2 0.7 copy-start.13
  73.0 1.0 copy-start.14
  74.8 1.0 copy-start.9
  75.8 0.6 copy-start.27
  76.4 30.9 %all-to-all-start.1 = ((bf16[8,512,128]{2,1,0:T(8,128)(2,1)}), bf16[8,512,128]{2,1,0:T(8,128)(2,1)S(1)}, u32[]{:S(2)}, u32[]{:S(2)}) async-start(bf16[8,512,128]{2,1,0:T(8,128)(2,1)} %copy-done.9), calls=%async_computation.1 | async-start | bytes 2097152 | tf_op jit(solution)/shard_map/all_to_all | solution.py:640
  80.8 2.5 %collective-permute-start.9 = (bf16[4,512,128]{2,1,0:T(8,128)(2,1)S(1)}, bf16[4,512,128]{2,1,0:T(8,128)(2,1)S(1)}, u32[]{:S(2)}, u32[]{:S(2)}) collective-permute-start(bf16[4,512,128]{2,1,0:T(8,128)(2,1)S(1)} %collective-permute-done.5.refs_4_.refs_7_.refs_11_.refs_15_.refs_19_), channel_id=1, source_target_pairs={{0,1},{1,0},{2,3},{3,2},{4,5},{5,4},{6,7},{7,6},{8,9},{9,8},{10,11... | collective-permute-start | bytes 1572872 | tf_op jit(solution)/shard_map/ppermute | solution.py:637
  80.8 0.6 copy-start.24
  81.4 0.7 copy-start.28
  82.6 2.1 %collective-permute-start.8 = (bf16[2,2,128,512]{3,2,1,0:T(8,128)(2,1)S(1)}, bf16[2,2,128,512]{3,2,1,0:T(8,128)(2,1)S(1)}, u32[]{:S(2)}, u32[]{:S(2)}) collective-permute-start(bf16[2,2,128,512]{3,2,1,0:T(8,128)(2,1)S(1)} %pair.1), channel_id=1, source_target_pairs={{0,1},{1,0},{2,3},{3,2},{4,5},{5,4},{6,7},{7,6},{8,9},{9,8},{10,11... | collective-permute-start | bytes 1572872 | tf_op jit(solution)/shard_map/ppermute | solution.py:637
  84.7 1.2 %copy-start.8 = (bf16[1,128,4096]{2,1,0:T(8,128)(2,1)S(1)}, bf16[1,128,4096]{2,1,0:T(8,128)(2,1)}, u32[]{:S(2)}) copy-start(bf16[1,128,4096]{2,1,0:T(8,128)(2,1)} %param.27) | copy-start | bytes 3145732
  86.0 0.6 copy-start.25
  86.6 0.7 copy-start.29
  87.3 0.7 copy-start.30
  88.0 0.7 copy-start.31
  106.6 0.6 copy-start.32
  107.2 1.1 copy-start.5
  108.3 1.1 copy-start.7
  109.3 0.6 copy-start.26
  109.9 0.7 copy-start.33
  110.6 3.9 %copy-start.20 = (bf16[1,128,64]{1,2,0:T(8,128)(2,1)S(1)}, bf16[1,128,64]{1,2,0:T(8,128)(2,1)}, u32[]{:S(2)}) copy-start(bf16[1,128,64]{1,2,0:T(8,128)(2,1)} %param.18) | copy-start | bytes 49156
  111.7 2.7 %collective-permute-start.10 = (bf16[8,512,128]{2,1,0:T(8,128)(2,1)S(1)}, bf16[8,512,128]{2,1,0:T(8,128)(2,1)S(1)}, u32[]{:S(2)}, u32[]{:S(2)}) collective-permute-start(bf16[8,512,128]{2,1,0:T(8,128)(2,1)S(1)} %get-tuple-element.30), channel_id=1, source_target_pairs={{0,1},{1,0},{2,3},{3,2},{4,5},{5,4},{6,7},{7,6},{8,9},{9,8},{10,11... | collective-permute-start | bytes 3145736 | tf_op jit(solution)/shard_map/ppermute | solution.py:637
  114.5 2.2 %copy-start.2 = (f32[128,8192]{1,0:T(8,128)S(1)}, f32[128,8192]{1,0:T(8,128)}, u32[]{:S(2)}) copy-start(f32[128,8192]{1,0:T(8,128)} %copy-done.1) | copy-start | bytes 12582916
where the time goes:
time: 122 us; the launch traced here: 121 us
  Pallas kernels  41.4 us (34%)
  waiting for transfers between devices  28.8 us (24%)
  starting transfers between devices  27 us (22%)
  local copies, waits for them, and re-layouts  22.9 us (19%)
    ppermute x9, waiting for transfers between devices, apart(): lax.ppermute(block, 'ctx', [(i, i ^ distance) for i in range(devices)])  28.8 us
    unnamed x74, local copies, waits for them, and re-layouts  21.2 us
    pallas_call x1, Pallas kernels, attend(): pl.pallas_call(scalars(attend_kernel), out_shape=[jax.ShapeDtypeStruct((T...  18 us
    all_to_all x2, starting transfers between devices, exchanged(): lax.all_to_all(block, 'ctx', 0, 0, axis_index_groups=same_core, tiled=True)  11.2 us
    ppermute x9, starting transfers between devices, apart(): lax.ppermute(block, 'ctx', [(i, i ^ distance) for i in range(devices)])  9.88 us
    pallas_call x8, Pallas kernels, whole(): pl.pallas_call(kernel, out_shape=[jax.ShapeDtypeStruct(s, t) for s, t in...  9.7 us
    pallas_call x1, Pallas kernels, summaries(): pl.pallas_call(scalars(summary_kernel, local), out_shape=[shape, shape],...  5.24 us
    ppermute x1, starting transfers between devices, shifted(): lax.ppermute(block, axis, [(i - distance, i) for i in devices if i - dist...  4.5 us
  transfers between devices with their start and end apart: 13, of which 5 were waited for; matrix products, arithmetic and copies ran while one was open for 0% of the time, Pallas kernels for 21%

commit v1 on v0

--- a/solution.py
+++ b/solution.py
@@ -29,7 +29,7 @@
 COLUMNS = SPAN + 64
 NEG = -1e30
 TOKEN = jax.ShapeDtypeStruct((8, 128), jnp.float32)
-FREE = pl.CostEstimate(flops=1024, bytes_accessed=1024, transcendentals=0)
+LONG = pl.CostEstimate(flops=1 << 35, bytes_accessed=1 << 20, transcendentals=0)
 
 
 class Scalars:
@@ -64,7 +64,7 @@
     return body
 
 
-def params(mib=24):
+def params(mib=60):
     return pltpu.CompilerParams(vmem_limit_bytes=mib * 1024 * 1024)
 
 
@@ -155,8 +155,8 @@
                 pltpu.VMEM((G * N, TOK), jnp.float32),
             ],
         ),
-        compiler_params=params(60),
-        cost_estimate=FREE,
+        compiler_params=params(),
+        cost_estimate=LONG,
         name="summaries",
     )(meta, x, rates, steps, writes, idle)
 
@@ -165,7 +165,7 @@
     return pl.BlockSpec(memory_space=pl.ANY)
 
 
-def whole(kernel, name, meta, arrays, shapes, idle=(), mib=24, scratch=()):
+def whole(kernel, name, meta, arrays, shapes, idle=(), mib=60, scratch=()):
     def spec(shape):
         return pl.BlockSpec(shape, lambda i, *m: (0,) * len(shape))
 
@@ -180,7 +180,7 @@
             scratch_shapes=scratch,
         ),
         compiler_params=params(mib),
-        cost_estimate=FREE,
+        cost_estimate=LONG,
         name=name,
     )(meta, *arrays, *idle)
 
@@ -374,7 +374,7 @@
             ],
         ),
         compiler_params=params(),
-        cost_estimate=FREE,
+        cost_estimate=LONG,
         name="intra",
     )(meta, skip, x, rates, steps, writes, reads, idle)
 
@@ -440,7 +440,7 @@
             scratch_shapes=[pltpu.VMEM((H, TOK), jnp.float32)],
         ),
         compiler_params=params(),
-        cost_estimate=FREE,
+        cost_estimate=LONG,
         name="finish",
     )(meta, part, rates, steps, reads, own, other)
 
@@ -589,7 +589,7 @@
             ],
         ),
         compiler_params=params(),
-        cost_estimate=FREE,
+        cost_estimate=LONG,
         name="attend",
     )(
         meta, queries, *bands, *pieces, *pieces, *pieces, *pieces, sink_keys, sink_values, *idle
@@ -647,7 +647,6 @@
         meta,
         [cache_keys[0], cache_values[0], turn_keys[0], turn_values[0]],
         [(parcel, jnp.bfloat16), (parcel, jnp.bfloat16), (band, jnp.bfloat16)],
-        mib=60,
     )
     distance = devices // 2
     moved = apart(away, distance)
@@ -665,7 +664,7 @@
         meta,
         [near, moved, key_value, four],
         [joined(near), (band, jnp.bfloat16)],
-        idle=[send],
+        idle=[got],
     )
     distance //= 2
     moved = apart(near, distance)
@@ -682,26 +681,29 @@
     for j in range(1, groups):
         route = [((i + j) % groups, i) for i in range(groups)]
         stored.append(lax.ppermute(turned, "sess", route))
-    after = turned
-    while distance > 2:
-        [near] = whole(scalars(join_kernel), "join", meta, [near, moved], [joined(near)], idle=[after])
-        after = near
-        distance //= 2
-        moved = apart(near, distance)
-
+    two = apart(two, 2)
     [chip] = whole(
         scalars(combine_kernel, local),
         "combine",
         meta,
         [keep, got],
         [(keep.shape, jnp.bfloat16)],
-        idle=[after],
+        idle=[turned, two],
     )
     total = exchanged(chip)
+    [pair] = whole(
+        scalars(pair_kernel), "pair", meta, [key_value, two, four], [((2, *band), jnp.bfloat16)], idle=[chip]
+    )
+    after = pair
+    pair = apart(pair, 1)
+    while distance > 2:
+        [near] = whole(scalars(join_kernel), "join", meta, [near, moved], [joined(near)], idle=[after])
+        after = near
+        distance //= 2
+        moved = apart(near, distance)
     beside = moved
     across = apart(near, 1)
-    two = apart(two, 2)
-    part, token = intra(meta, skip_gain, x, rates, steps, writes, reads, chip)
+    part, token = intra(meta, skip_gain, x, rates, steps, writes, reads, after)
 
     entering, after = whole(
         scalars(recurrence_kernel, local, groups),
@@ -709,14 +711,10 @@
         meta,
         [total, *stored],
         [((chips, 2 * width, P_SIZE), jnp.bfloat16), (TOKEN.shape, TOKEN.dtype)],
-        idle=[token, beside, across, two],
+        idle=[token, beside, across, pair],
         scratch=[pltpu.VMEM((SEQS, width, P_SIZE), jnp.float32)],
     )
     entering = exchanged(entering)
-    [pair] = whole(
-        scalars(pair_kernel), "pair", meta, [key_value, two, four], [((2, *band), jnp.bfloat16)], idle=[after]
-    )
-    pair = apart(pair, 1)
     pieces = [near, beside, across, apart(beside, 1)]
     bands = [four, pair, two, pair, key_value]
     attended, token = attend(

time: 122 us -> 121 us (level)
  local copies, waits for them, and re-layouts: 22.9 us -> 9.14 us
  Pallas kernels: 41.4 us -> 55.1 us
    unnamed x74 -> x34, local copies, waits for them, and re-layouts: 21.2 us -> 6.56 us
    pallas_call x8, Pallas kernels: 9.7 us -> 23.3 us  [whole(): pl.pallas_call(kernel, out_shape=[jax.ShapeDtypeStruct(s, t) for s, t in...]
    ppermute x9, waiting for transfers between devices: 28.8 us -> 15.7 us  [apart(): lax.ppermute(block, 'ctx', [(i, i ^ distance) for i in range(devices)])]
    all_to_all x2, waiting for transfers between devices: 0.01 us -> 12 us  [exchanged(): lax.all_to_all(block, 'ctx', 0, 0, axis_index_groups=same_core, tiled=True)]
    pallas_call x1, Pallas kernels: 18 us -> 13.4 us  [attend(): pl.pallas_call(scalars(attend_kernel), out_shape=[jax.ShapeDtypeStruct((T...]
    pallas_call x1, Pallas kernels: 4.14 us -> 6.68 us  [intra(): pl.pallas_call(scalars(intra_kernel), out_shape=[jax.ShapeDtypeStruct((TO...]
    pallas_call x1, Pallas kernels: 4.3 us -> 6.47 us  [finish(): pl.pallas_call(scalars(finish_kernel, local), out_shape=jax.ShapeDtypeStr...]
    ppermute x9, starting transfers between devices: 9.88 us -> 11.1 us  [apart(): lax.ppermute(block, 'ctx', [(i, i ^ distance) for i in range(devices)])]
  transfers between devices with their start and end apart: 13 -> 13, of which waited for: 5 -> 5; matrix products, arithmetic and copies ran while one was open for 0% -> 1% of each run, Pallas kernels for 21% -> 29%
where the time goes in v1:
time: 121 us; the launch traced here: 120 us
  Pallas kernels  55.1 us (46%)
  waiting for transfers between devices  27.6 us (23%)
  starting transfers between devices  27.1 us (22%)
  local copies, waits for them, and re-layouts  9.14 us (8%)
    pallas_call x8, Pallas kernels, whole(): pl.pallas_call(kernel, out_shape=[jax.ShapeDtypeStruct(s, t) for s, t in...  23.3 us
    ppermute x9, waiting for transfers between devices, apart(): lax.ppermute(block, 'ctx', [(i, i ^ distance) for i in range(devices)])  15.7 us
    pallas_call x1, Pallas kernels, attend(): pl.pallas_call(scalars(attend_kernel), out_shape=[jax.ShapeDtypeStruct((T...  13.4 us
    all_to_all x2, waiting for transfers between devices, exchanged(): lax.all_to_all(block, 'ctx', 0, 0, axis_index_groups=same_core, tiled=True)  12 us
    ppermute x9, starting transfers between devices, apart(): lax.ppermute(block, 'ctx', [(i, i ^ distance) for i in range(devices)])  11.1 us
    all_to_all x2, starting transfers between devices, exchanged(): lax.all_to_all(block, 'ctx', 0, 0, axis_index_groups=same_core, tiled=True)  10 us
    pallas_call x1, Pallas kernels, intra(): pl.pallas_call(scalars(intra_kernel), out_shape=[jax.ShapeDtypeStruct((TO...  6.68 us
    unnamed x34, local copies, waits for them, and re-layouts  6.56 us
  transfers between devices with their start and end apart: 13, of which 5 were waited for; matrix products, arithmetic and copies ran while one was open for 1% of the time, Pallas kernels for 29%

profile of v1, /device:TPU:0, one launch (start us, length us, event | category | flops | bytes accessed | tf_op | source)
XLA Modules:
  0.0 119.8 jit_solution(14291355747103770419)
XLA Ops:
  0.6 1.3 %concatenate.3.ids = s32[14]{0:T(128)} concatenate(s32[1]{0:T(128)} %bitcast, s32[1]{0:T(128)} %bitcast.1, s32[3]{0:T(128)} %bitcast.22, s32[3]{0:T(128)} %bitcast.23, s32[6]{0:T(128)} %param.24), dimensions={0} | concatenate | bytes 112 | tf_op jit(solution)/shard_map/concatenate | solution.py:631
  1.9 2.5 %pack.1 = (bf16[1,512,128]{2,1,0:T(8,128)(2,1)}, bf16[1,512,128]{2,1,0:T(8,128)(2,1)}, bf16[2,128,512]{2,1,0:T(8,128)(2,1)}) custom-call(s32[14]{0:T(128)} %concatenate.3.ids, bf16[3,32,512]{2,1,0:T(8,128)(2,1)} %bitcast.33, bf16[3,32,512]{2,1,0:T(8,128)(2,1)} %bitcast.34, bf16[128,512]{1,0:T(8,128)(2,1)} %bitcast.27, bf16[128,512]{1,0:T(8,128)(2,1)} %bitcast.28), custom_call_target="tpu_custom_call" | custom-call | flops 34359738368 | bytes 1048576 | tf_op jit(solution)/shard_map/pack/pallas_call | solution.py:172
  4.5 0.0 copy-start.11
  4.5 5.2 %summaries.1 = (bf16[8,272,128]{2,1,0:T(8,128)(2,1)}, bf16[8,272,128]{2,1,0:T(8,128)(2,1)}) custom-call(s32[14]{0:T(128)} %concatenate.3.ids, bf16[128,8192]{1,0:T(8,128)(2,1)} %bitcast.24, bf16[64,128]{1,0:T(8,128)(2,1)} %bitcast.35, bf16[64,128]{1,0:T(8,128)(2,1)} %bitcast.38, bf16[128,512]{1,0:T(8,128)(2,1)} %bitcast.29, ...), custom_call_target="tpu_custom_call" | custom-call | flops 34359738368 | bytes 1048576 | tf_op jit(solution)/shard_map/summaries/pallas_call | solution.py:138
  9.7 0.5 collective-permute-start.2
  10.2 0.0 copy-done.11
  10.2 4.5 %collective-permute-start.1 = (bf16[2,128,512]{2,1,0:T(8,128)(2,1)S(1)}, bf16[2,128,512]{2,1,0:T(8,128)(2,1)S(1)}, u32[]{:S(2)}, u32[]{:S(2)}) collective-permute-start(bf16[2,128,512]{2,1,0:T(8,128)(2,1)S(1)} %copy-done.11), channel_id=1, source_target_pairs={{0,4},{1,5},{2,6},{3,7},{4,8},{5,9},{6,10},{7,11},{8,12},{9,13},{1... | collective-permute-start | bytes 786440 | tf_op jit(solution)/shard_map/ppermute | solution.py:601
  14.7 0.0 copy-done.15
  14.7 2.6 %collective-permute-start = (bf16[1,512,128]{2,1,0:T(8,128)(2,1)S(1)}, bf16[1,512,128]{2,1,0:T(8,128)(2,1)S(1)}, u32[]{:S(2)}, u32[]{:S(2)}) collective-permute-start(bf16[1,512,128]{2,1,0:T(8,128)(2,1)S(1)} %copy-done.15), channel_id=1, source_target_pairs={{0,8},{1,9},{2,10},{3,11},{4,12},{5,13},{6,14},{7,15},{8,0},{9,1},... | collective-permute-start | bytes 393224 | tf_op jit(solution)/shard_map/ppermute | solution.py:637
  17.3 0.0 copy-done.2
  17.3 1.3 %reshape_squeeze.3.refs_0_ = f32[3,4,128,64]{3,2,1,0:T(8,128)} reshape(f32[1,3,4,8192]{3,2,1,0:T(4,128)S(1)} %copy-done.2) | data formatting | bytes 786432 | tf_op jit(solution)/shard_map/reshape;squeeze | solution.py:676
  18.6 5.5 %collective-permute-done.refs_1_ = bf16[1,512,128]{2,1,0:T(8,128)(2,1)S(1)} collective-permute-done((bf16[1,512,128]{2,1,0:T(8,128)(2,1)S(1)}, bf16[1,512,128]{2,1,0:T(8,128)(2,1)S(1)}, u32[]{:S(2)}, u32[]{:S(2)}) %collective-permute-start) | collective-permute-done | bytes 131104 | tf_op jit(solution)/shard_map/ppermute | solution.py:637
  24.1 0.0 collective-permute-done.1.refs_3_.refs_2_.refs_1_
  24.1 0.0 collective-permute-done.2.refs_4_.refs_1_.refs_2_
  24.1 0.0 copy-start.4
  24.1 0.6 copy-done.16
  24.7 0.1 copy-done.12
  24.9 0.2 copy-done.4
  25.0 2.6 %join_two.1 = (bf16[2,512,128]{2,1,0:T(8,128)(2,1)}, bf16[2,128,512]{2,1,0:T(8,128)(2,1)}) custom-call(s32[14]{0:T(128)} %concatenate.3.ids, bf16[1,512,128]{2,1,0:T(8,128)(2,1)} %get-tuple-element.17.refs_0_, bf16[1,512,128]{2,1,0:T(8,128)(2,1)} %copy-done.16, bf16[2,128,512]{2,1,0:T(8,128)(2,1)} %get-tuple-element.19.refs_2_.refs_0_.refs_5_, ...), custom_call_target="tpu_custom_call" | custom-call | flops 34359738368 | bytes 1048576 | tf_op jit(solution)/shard_map/join_two/pallas_call | solution.py:172
  27.7 4.0 %collective-permute-start.3 = (bf16[2,512,128]{2,1,0:T(8,128)(2,1)}, bf16[2,512,128]{2,1,0:T(8,128)(2,1)S(1)}, u32[]{:S(2)}, u32[]{:S(2)}) collective-permute-start(bf16[2,512,128]{2,1,0:T(8,128)(2,1)} %get-tuple-element.21.refs_0_), channel_id=1, source_target_pairs={{0,4},{1,5},{2,6},{3,7},{4,0},{5,1},{6,2},{7,3},{8,12},{9,13},{10,... | collective-permute-start | bytes 786440 | tf_op jit(solution)/shard_map/ppermute | solution.py:637
  31.7 1.5 %collective-permute-start.4 = (bf16[2,128,512]{2,1,0:T(8,128)(2,1)}, bf16[2,128,512]{2,1,0:T(8,128)(2,1)S(1)}, u32[]{:S(2)}, u32[]{:S(2)}) collective-permute-start(bf16[2,128,512]{2,1,0:T(8,128)(2,1)} %get-tuple-element.22.refs_1_), channel_id=1, source_target_pairs={{0,2},{1,3},{2,0},{3,1},{4,6},{5,7},{6,4},{7,5},{8,10},{9,11},{10,... | collective-permute-start | bytes 786440 | tf_op jit(solution)/shard_map/ppermute | solution.py:637
  33.2 2.8 %turn.1.refs_2_.refs_1_ = f32[3,256,128]{2,1,0:T(8,128)} custom-call(s32[14]{0:T(128)} %concatenate.3.ids, f32[3,4,128,64]{3,2,1,0:T(8,128)} %reshape_squeeze.3.refs_0_, bf16[2,128,512]{2,1,0:T(8,128)(2,1)} %get-tuple-element.22.refs_1_), custom_call_target="tpu_custom_call" | custom-call | flops 34359738368 | bytes 1048576 | tf_op jit(solution)/shard_map/turn/pallas_call | solution.py:172
  36.0 1.5 %collective-permute-start.5 = (f32[3,256,128]{2,1,0:T(8,128)}, f32[3,256,128]{2,1,0:T(8,128)S(1)}, u32[]{:S(2)}, u32[]{:S(2)}) collective-permute-start(f32[3,256,128]{2,1,0:T(8,128)} %turn.1.refs_2_.refs_1_), channel_id=1, source_target_pairs={{16,0},{0,16},{17,1},{1,17},{18,2},{2,18},{19,3},{3,19},{20,4},{4,... | collective-permute-start | bytes 1179656 | tf_op jit(solution)/shard_map/ppermute | solution.py:683
  37.5 2.0 %collective-permute-done.4.refs_3_.refs_1_ = bf16[2,128,512]{2,1,0:T(8,128)(2,1)S(1)} collective-permute-done((bf16[2,128,512]{2,1,0:T(8,128)(2,1)}, bf16[2,128,512]{2,1,0:T(8,128)(2,1)S(1)}, u32[]{:S(2)}, u32[]{:S(2)}) %collective-permute-start.4) | collective-permute-done | bytes 262176 | tf_op jit(solution)/shard_map/ppermute | solution.py:637
  39.5 0.7 copy-done.13
  40.2 2.9 %combine.1.refs_3_ = bf16[8,272,128]{2,1,0:T(8,128)(2,1)} custom-call(s32[14]{0:T(128)} %concatenate.3.ids, bf16[8,272,128]{2,1,0:T(8,128)(2,1)} %get-tuple-element.23.refs_0_.refs_1_, bf16[8,272,128]{2,1,0:T(8,128)(2,1)} %copy-done.4, f32[3,256,128]{2,1,0:T(8,128)} %turn.1.refs_2_.refs_1_, bf16[2,128,512]{2,1,0:T(8,128)(2,1)} %copy-done.13), custom_call_target="tpu_custom_call" | custom-call | flops 34359738368 | bytes 1048576 | tf_op jit(solution)/shard_map/combine/pallas_call | solution.py:172
  43.2 5.6 %all-to-all-start = ((bf16[8,272,128]{2,1,0:T(8,128)(2,1)}), bf16[8,272,128]{2,1,0:T(8,128)(2,1)S(1)}, u32[]{:S(2)}, u32[]{:S(2)}) async-start(bf16[8,272,128]{2,1,0:T(8,128)(2,1)} %combine.1.refs_3_), calls=%async_computation | async-start | bytes 1114112 | tf_op jit(solution)/shard_map/all_to_all | solution.py:640
  48.8 2.6 %pair.1.refs_2_ = bf16[2,2,128,512]{3,2,1,0:T(8,128)(2,1)} custom-call(s32[14]{0:T(128)} %concatenate.3.ids, bf16[2,128,512]{2,1,0:T(8,128)(2,1)} %get-tuple-element.19.refs_2_.refs_0_.refs_5_, bf16[2,128,512]{2,1,0:T(8,128)(2,1)} %copy-done.13, bf16[2,128,512]{2,1,0:T(8,128)(2,1)} %copy-done.12, bf16[8,272,128]{2,1,0:T(8,128)(2,1)} %combine.1.refs_3_), custom_call_target="tpu_custom_call" | custom-call | flops 34359738368 | bytes 1048576 | tf_op jit(solution)/shard_map/pair/pallas_call | solution.py:172
  51.4 0.0 collective-permute-done.3.refs_1_
  51.4 0.7 copy-done.14
  52.1 2.5 %join.1.refs_6_.refs_10_.refs_14_.refs_18_ = bf16[4,512,128]{2,1,0:T(8,128)(2,1)} custom-call(s32[14]{0:T(128)} %concatenate.3.ids, bf16[2,512,128]{2,1,0:T(8,128)(2,1)} %get-tuple-element.21.refs_0_, bf16[2,512,128]{2,1,0:T(8,128)(2,1)} %copy-done.14, bf16[2,2,128,512]{3,2,1,0:T(8,128)(2,1)} %pair.1.refs_2_), custom_call_target="tpu_custom_call" | custom-call | flops 34359738368 | bytes 1048576 | tf_op jit(solution)/shard_map/join/pallas_call | solution.py:172
  54.6 2.0 %collective-permute-start.6 = (bf16[4,512,128]{2,1,0:T(8,128)(2,1)}, bf16[4,512,128]{2,1,0:T(8,128)(2,1)S(1)}, u32[]{:S(2)}, u32[]{:S(2)}) collective-permute-start(bf16[4,512,128]{2,1,0:T(8,128)(2,1)} %join.1.refs_6_.refs_10_.refs_14_.refs_18_), channel_id=1, source_target_pairs={{0,2},{1,3},{2,0},{3,1},{4,6},{5,7},{6,4},{7,5},{8,10},{9,11},{10,... | collective-permute-start | bytes 1572872 | tf_op jit(solution)/shard_map/ppermute | solution.py:637
  56.6 0.0 collective-permute-start.7
  56.7 0.0 copy-done.9
  56.7 0.5 collective-permute-start.8
  57.2 6.7 %intra.1 = (f32[128,8192]{1,0:T(8,128)}, f32[8,128]{1,0:T(8,128)}) custom-call(s32[14]{0:T(128)} %concatenate.3.ids, f32[64]{0:T(128)} %refs_0_.1, bf16[128,8192]{1,0:T(8,128)(2,1)} %bitcast.25, bf16[64,128]{1,0:T(8,128)(2,1)} %bitcast.36, bf16[64,128]{1,0:T(8,128)(2,1)} %bitcast.39, bf16[128,512]{1,0:T(8,128)(2,1)} %bitcast.30, bf16[128,512]{1,0:T(8,128)(2,1)} %bitcast.31, ...), custom_call_target="tpu_custom_call" | custom-call | flops 34359738368 | bytes 1048576 | tf_op jit(solution)/shard_map/intra/pallas_call | solution.py:353
  63.8 5.3 %collective-permute-done.6.refs_4_.refs_7_.refs_11_.refs_15_.refs_19_ = bf16[4,512,128]{2,1,0:T(8,128)(2,1)S(1)} collective-permute-done((bf16[4,512,128]{2,1,0:T(8,128)(2,1)}, bf16[4,512,128]{2,1,0:T(8,128)(2,1)S(1)}, u32[]{:S(2)}, u32[]{:S(2)}) %collective-permute-start.6) | collective-permute-done | bytes 524320 | tf_op jit(solution)/shard_map/ppermute | solution.py:637
  69.2 0.0 collective-permute-start.9
  69.2 0.0 collective-permute-done.5.refs_2_
  69.2 0.0 copy-start.10
  69.2 0.0 collective-permute-done.7.refs_5_.refs_8_.refs_12_.refs_16_.refs_20_
  69.2 0.0 copy-start.6
  69.2 0.0 collective-permute-done.8.refs_6_.refs_2_.refs_4_
  69.2 0.0 copy-start.7
  69.2 0.0 all-to-all-done.refs_0_
  69.2 0.0 copy-start.1
  69.2 0.7 copy-done.5
  70.0 0.2 copy-done.10
  70.2 0.2 copy-done.6
  70.3 0.2 copy-done.7
  70.5 0.1 copy-done.1
  70.6 3.2 %recurrence.1 = (bf16[8,512,128]{2,1,0:T(8,128)(2,1)}, f32[8,128]{1,0:T(8,128)}) custom-call(s32[14]{0:T(128)} %concatenate.3.ids, bf16[8,272,128]{2,1,0:T(8,128)(2,1)} %copy-done.1, f32[3,256,128]{2,1,0:T(8,128)} %turn.1.refs_2_.refs_1_, f32[3,256,128]{2,1,0:T(8,128)} %copy-done.10, f32[8,128]{1,0:T(8,128)} %get-tuple-element.25.refs_3_, ...), custom_call_target="tpu_custom_call" | custom-call | flops 34359738368 | bytes 1048576 | tf_op jit(solution)/shard_map/recurrence/pallas_call | solution.py:172
  73.8 4.4 %all-to-all-start.1 = ((bf16[8,512,128]{2,1,0:T(8,128)(2,1)}), bf16[8,512,128]{2,1,0:T(8,128)(2,1)S(1)}, u32[]{:S(2)}, u32[]{:S(2)}) async-start(bf16[8,512,128]{2,1,0:T(8,128)(2,1)} %get-tuple-element.26), calls=%async_computation.1 | async-start | bytes 2097152 | tf_op jit(solution)/shard_map/all_to_all | solution.py:640
  78.2 0.0 collective-permute-done.9.refs_9_.refs_13_.refs_17_.refs_21_
  78.2 0.0 copy-start.8
  78.2 0.8 copy-done.8
  79.0 13.4 %attend.1 = (bf16[128,4096]{1,0:T(8,128)(2,1)}, f32[8,128]{1,0:T(8,128)}) custom-call(s32[14]{0:T(128)} %concatenate.3.ids, bf16[128,4096]{1,0:T(8,128)(2,1)} %bitcast.26, bf16[2,128,512]{2,1,0:T(8,128)(2,1)} %copy-done.12, bf16[2,2,128,512]{3,2,1,0:T(8,128)(2,1)} %copy-done.7, bf16[2,128,512]{2,1,0:T(8,128)(2,1)} %copy-done.13, ...), custom_call_target="tpu_custom_call" | custom-call | flops 34359738368 | bytes 1048576 | tf_op jit(solution)/shard_map/attend/pallas_call | solution.py:568
  92.5 12.0 %all-to-all-done.1.refs_0_ = bf16[8,512,128]{2,1,0:T(8,128)(2,1)S(1)} async-done(((bf16[8,512,128]{2,1,0:T(8,128)(2,1)}), bf16[8,512,128]{2,1,0:T(8,128)(2,1)S(1)}, u32[]{:S(2)}, u32[]{:S(2)}) %all-to-all-start.1) | async-done | bytes 1048608 | tf_op jit(solution)/shard_map/all_to_all | solution.py:640
  104.5 1.0 copy-done
  105.4 4.1 %middle.1 = (bf16[8,512,128]{2,1,0:T(8,128)(2,1)}, bf16[8,512,128]{2,1,0:T(8,128)(2,1)}) custom-call(s32[14]{0:T(128)} %concatenate.3.ids, bf16[8,512,128]{2,1,0:T(8,128)(2,1)} %copy-done, bf16[8,272,128]{2,1,0:T(8,128)(2,1)} %get-tuple-element.23.refs_0_.refs_1_, bf16[8,272,128]{2,1,0:T(8,128)(2,1)} %copy-done.4, f32[8,128]{1,0:T(8,128)} %get-tuple-element.28.refs_3_), custom_call_target="tpu_custom_call" | custom-call | flops 34359738368 | bytes 1048576 | tf_op jit(solution)/shard_map/middle/pallas_call | solution.py:172
  109.5 0.0 collective-permute-start.10
  109.5 2.9 %collective-permute-done.10.refs_5_ = bf16[8,512,128]{2,1,0:T(8,128)(2,1)S(1)} collective-permute-done((bf16[8,512,128]{2,1,0:T(8,128)(2,1)}, bf16[8,512,128]{2,1,0:T(8,128)(2,1)S(1)}, u32[]{:S(2)}, u32[]{:S(2)}) %collective-permute-start.10) | collective-permute-done | bytes 1048608 | tf_op jit(solution)/shard_map/ppermute | solution.py:637
  112.4 1.0 copy-done.3
  113.4 6.5 %finish.1 = bf16[128,8192]{1,0:T(8,128)(2,1)} custom-call(s32[14]{0:T(128)} %concatenate.3.ids, f32[128,8192]{1,0:T(8,128)} %get-tuple-element.24.refs_0_, bf16[64,128]{1,0:T(8,128)(2,1)} %bitcast.37, bf16[64,128]{1,0:T(8,128)(2,1)} %bitcast.40, bf16[128,512]{1,0:T(8,128)(2,1)} %bitcast.32, bf16[8,512,128]{2,1,0:T(8,128)(2,1)} %get-tuple-element.29.refs_4_, ...), custom_call_target="tpu_custom_call" | custom-call | flops 34359738368 | bytes 1048576 | tf_op jit(solution)/shard_map/finish/pallas_call | solution.py:425
  (10 shorter events, 0.0 us)
Async XLA Ops:
  4.5 5.7 %copy-start.11 = (bf16[2,128,512]{2,1,0:T(8,128)(2,1)S(1)}, bf16[2,128,512]{2,1,0:T(8,128)(2,1)}, u32[]{:S(2)}) copy-start(bf16[2,128,512]{2,1,0:T(8,128)(2,1)} %get-tuple-element.19.refs_2_.refs_0_.refs_5_) | copy-start | bytes 786436
  4.5 10.2 %copy-start.15 = (bf16[1,512,128]{2,1,0:T(8,128)(2,1)S(1)}, bf16[1,512,128]{2,1,0:T(8,128)(2,1)}, u32[]{:S(2)}) copy-start(bf16[1,512,128]{2,1,0:T(8,128)(2,1)} %get-tuple-element.18.refs_4_) | copy-start | bytes 393220
  4.5 12.9 %copy-start.2 = (f32[1,3,4,8192]{3,2,1,0:T(4,128)S(1)}, f32[1,3,4,8192]{3,2,1,0:T(4,128)}, u32[]{:S(2)}) copy-start(f32[1,3,4,8192]{3,2,1,0:T(4,128)} %param.23) | copy-start | bytes 1179652
  9.7 14.4 %collective-permute-start.2 = (bf16[8,272,128]{2,1,0:T(8,128)(2,1)}, bf16[8,272,128]{2,1,0:T(8,128)(2,1)S(1)}, u32[]{:S(2)}, u32[]{:S(2)}) collective-permute-start(bf16[8,272,128]{2,1,0:T(8,128)(2,1)} %get-tuple-element.20), channel_id=1, source_target_pairs={{0,1},{1,0},{2,3},{3,2},{4,5},{5,4},{6,7},{7,6},{8,9},{9,8},{10,11... | collective-permute-start | bytes 1671176 | tf_op jit(solution)/shard_map/ppermute | solution.py:637
  10.2 13.9 %collective-permute-start.1 = (bf16[2,128,512]{2,1,0:T(8,128)(2,1)S(1)}, bf16[2,128,512]{2,1,0:T(8,128)(2,1)S(1)}, u32[]{:S(2)}, u32[]{:S(2)}) collective-permute-start(bf16[2,128,512]{2,1,0:T(8,128)(2,1)S(1)} %copy-done.11), channel_id=1, source_target_pairs={{0,4},{1,5},{2,6},{3,7},{4,8},{5,9},{6,10},{7,11},{8,12},{9,13},{1... | collective-permute-start | bytes 786440 | tf_op jit(solution)/shard_map/ppermute | solution.py:601
  14.7 9.4 %collective-permute-start = (bf16[1,512,128]{2,1,0:T(8,128)(2,1)S(1)}, bf16[1,512,128]{2,1,0:T(8,128)(2,1)S(1)}, u32[]{:S(2)}, u32[]{:S(2)}) collective-permute-start(bf16[1,512,128]{2,1,0:T(8,128)(2,1)S(1)} %copy-done.15), channel_id=1, source_target_pairs={{0,8},{1,9},{2,10},{3,11},{4,12},{5,13},{6,14},{7,15},{8,0},{9,1},... | collective-permute-start | bytes 393224 | tf_op jit(solution)/shard_map/ppermute | solution.py:637
  24.1 0.7 copy-start.16
  24.1 0.8 copy-start.12
  24.1 0.9 copy-start.4
  27.7 23.7 %collective-permute-start.3 = (bf16[2,512,128]{2,1,0:T(8,128)(2,1)}, bf16[2,512,128]{2,1,0:T(8,128)(2,1)S(1)}, u32[]{:S(2)}, u32[]{:S(2)}) collective-permute-start(bf16[2,512,128]{2,1,0:T(8,128)(2,1)} %get-tuple-element.21.refs_0_), channel_id=1, source_target_pairs={{0,4},{1,5},{2,6},{3,7},{4,0},{5,1},{6,2},{7,3},{8,12},{9,13},{10,... | collective-permute-start | bytes 786440 | tf_op jit(solution)/shard_map/ppermute | solution.py:637
  31.7 7.9 %collective-permute-start.4 = (bf16[2,128,512]{2,1,0:T(8,128)(2,1)}, bf16[2,128,512]{2,1,0:T(8,128)(2,1)S(1)}, u32[]{:S(2)}, u32[]{:S(2)}) collective-permute-start(bf16[2,128,512]{2,1,0:T(8,128)(2,1)} %get-tuple-element.22.refs_1_), channel_id=1, source_target_pairs={{0,2},{1,3},{2,0},{3,1},{4,6},{5,7},{6,4},{7,5},{8,10},{9,11},{10,... | collective-permute-start | bytes 786440 | tf_op jit(solution)/shard_map/ppermute | solution.py:637
  36.0 33.2 %collective-permute-start.5 = (f32[3,256,128]{2,1,0:T(8,128)}, f32[3,256,128]{2,1,0:T(8,128)S(1)}, u32[]{:S(2)}, u32[]{:S(2)}) collective-permute-start(f32[3,256,128]{2,1,0:T(8,128)} %turn.1.refs_2_.refs_1_), channel_id=1, source_target_pairs={{16,0},{0,16},{17,1},{1,17},{18,2},{2,18},{19,3},{3,19},{20,4},{4,... | collective-permute-start | bytes 1179656 | tf_op jit(solution)/shard_map/ppermute | solution.py:683
  39.5 0.7 copy-start.13
  43.2 26.1 %all-to-all-start = ((bf16[8,272,128]{2,1,0:T(8,128)(2,1)}), bf16[8,272,128]{2,1,0:T(8,128)(2,1)S(1)}, u32[]{:S(2)}, u32[]{:S(2)}) async-start(bf16[8,272,128]{2,1,0:T(8,128)(2,1)} %combine.1.refs_3_), calls=%async_computation | async-start | bytes 1114112 | tf_op jit(solution)/shard_map/all_to_all | solution.py:640
  51.4 5.3 %copy-start.9 = (bf16[2,2,128,512]{3,2,1,0:T(8,128)(2,1)S(1)}, bf16[2,2,128,512]{3,2,1,0:T(8,128)(2,1)}, u32[]{:S(2)}) copy-start(bf16[2,2,128,512]{3,2,1,0:T(8,128)(2,1)} %pair.1.refs_2_) | copy-start | bytes 1572868
  51.4 0.7 copy-start.14
  54.6 14.5 %collective-permute-start.6 = (bf16[4,512,128]{2,1,0:T(8,128)(2,1)}, bf16[4,512,128]{2,1,0:T(8,128)(2,1)S(1)}, u32[]{:S(2)}, u32[]{:S(2)}) collective-permute-start(bf16[4,512,128]{2,1,0:T(8,128)(2,1)} %join.1.refs_6_.refs_10_.refs_14_.refs_18_), channel_id=1, source_target_pairs={{0,2},{1,3},{2,0},{3,1},{4,6},{5,7},{6,4},{7,5},{8,10},{9,11},{10,... | collective-permute-start | bytes 1572872 | tf_op jit(solution)/shard_map/ppermute | solution.py:637
  56.6 12.5 %collective-permute-start.7 = (bf16[4,512,128]{2,1,0:T(8,128)(2,1)}, bf16[4,512,128]{2,1,0:T(8,128)(2,1)S(1)}, u32[]{:S(2)}, u32[]{:S(2)}) collective-permute-start(bf16[4,512,128]{2,1,0:T(8,128)(2,1)} %join.1.refs_6_.refs_10_.refs_14_.refs_18_), channel_id=1, source_target_pairs={{0,1},{1,0},{2,3},{3,2},{4,5},{5,4},{6,7},{7,6},{8,9},{9,8},{10,11... | collective-permute-start | bytes 1572872 | tf_op jit(solution)/shard_map/ppermute | solution.py:637
  56.7 12.5 %collective-permute-start.8 = (bf16[2,2,128,512]{3,2,1,0:T(8,128)(2,1)S(1)}, bf16[2,2,128,512]{3,2,1,0:T(8,128)(2,1)S(1)}, u32[]{:S(2)}, u32[]{:S(2)}) collective-permute-start(bf16[2,2,128,512]{3,2,1,0:T(8,128)(2,1)S(1)} %copy-done.9), channel_id=1, source_target_pairs={{0,1},{1,0},{2,3},{3,2},{4,5},{5,4},{6,7},{7,6},{8,9},{9,8},{10,11... | collective-permute-start | bytes 1572872 | tf_op jit(solution)/shard_map/ppermute | solution.py:637
  69.2 0.8 copy-start.5
  69.2 9.0 %collective-permute-start.9 = (bf16[4,512,128]{2,1,0:T(8,128)(2,1)S(1)}, bf16[4,512,128]{2,1,0:T(8,128)(2,1)S(1)}, u32[]{:S(2)}, u32[]{:S(2)}) collective-permute-start(bf16[4,512,128]{2,1,0:T(8,128)(2,1)S(1)} %collective-permute-done.6.refs_4_.refs_7_.refs_11_.refs_15_.refs_19_), channel_id=1, source_target_pairs={{0,1},{1,0},{2,3},{3,2},{4,5},{5,4},{6,7},{7,6},{8,9},{9,8},{10,11... | collective-permute-start | bytes 1572872 | tf_op jit(solution)/shard_map/ppermute | solution.py:637
  69.2 1.0 copy-start.10
  69.2 1.1 copy-start.6
  69.2 1.3 %copy-start.7 = (bf16[2,2,128,512]{3,2,1,0:T(8,128)(2,1)}, bf16[2,2,128,512]{3,2,1,0:T(8,128)(2,1)S(1)}, u32[]{:S(2)}) copy-start(bf16[2,2,128,512]{3,2,1,0:T(8,128)(2,1)S(1)} %collective-permute-done.8.refs_6_.refs_2_.refs_4_) | copy-start | bytes 1572868
  69.2 1.4 %copy-start.1 = (bf16[8,272,128]{2,1,0:T(8,128)(2,1)}, bf16[8,272,128]{2,1,0:T(8,128)(2,1)S(1)}, u32[]{:S(2)}) copy-start(bf16[8,272,128]{2,1,0:T(8,128)(2,1)S(1)} %all-to-all-done.refs_0_) | copy-start | bytes 1671172
  73.8 30.7 %all-to-all-start.1 = ((bf16[8,512,128]{2,1,0:T(8,128)(2,1)}), bf16[8,512,128]{2,1,0:T(8,128)(2,1)S(1)}, u32[]{:S(2)}, u32[]{:S(2)}) async-start(bf16[8,512,128]{2,1,0:T(8,128)(2,1)} %get-tuple-element.26), calls=%async_computation.1 | async-start | bytes 2097152 | tf_op jit(solution)/shard_map/all_to_all | solution.py:640
  78.2 0.9 copy-start.8
  104.5 1.0 copy-start
  109.5 2.9 %collective-permute-start.10 = (bf16[8,512,128]{2,1,0:T(8,128)(2,1)}, bf16[8,512,128]{2,1,0:T(8,128)(2,1)S(1)}, u32[]{:S(2)}, u32[]{:S(2)}) collective-permute-start(bf16[8,512,128]{2,1,0:T(8,128)(2,1)} %get-tuple-element.30), channel_id=1, source_target_pairs={{0,1},{1,0},{2,3},{3,2},{4,5},{5,4},{6,7},{7,6},{8,9},{9,8},{10,11... | collective-permute-start | bytes 3145736 | tf_op jit(solution)/shard_map/ppermute | solution.py:637
  112.4 1.0 copy-start.3

commit v2 on v1

--- a/solution.py
+++ b/solution.py
@@ -165,7 +165,7 @@
     return pl.BlockSpec(memory_space=pl.ANY)
 
 
-def whole(kernel, name, meta, arrays, shapes, idle=(), mib=60, scratch=()):
+def whole(kernel, name, meta, arrays, shapes, idle=(), mib=16, scratch=()):
     def spec(shape):
         return pl.BlockSpec(shape, lambda i, *m: (0,) * len(shape))
 
@@ -218,13 +218,6 @@
     out_ref[:count] = first_ref[...]
     out_ref[count:] = second_ref[...]
     two_ref[...] = jnp.where(meta.place // 2 % 2 == 0, key_value_ref[...], four_ref[...])
-
-
-def pair_kernel(meta, key_value_ref, two_ref, four_ref, *refs):
-    out_ref = refs[-1]
-    key_value, two, four = key_value_ref[...], two_ref[...], four_ref[...]
-    out_ref[0] = jnp.where(meta.even, key_value, two)
-    out_ref[1] = jnp.where(meta.even, two, four)
 
 
 def far_place(distance, bits):
@@ -254,9 +247,8 @@
             out_ref[chip, rows, :] = (carry[k : k + 1] * s0 + s1).astype(jnp.bfloat16)
 
 
-def recurrence_kernel(local, groups, meta, got_ref, *refs):
-    stored, (out_ref, token_ref, restored_ref) = refs[:groups], refs[-3:]
-    token_ref[...] = jnp.zeros_like(token_ref)
+def restore_kernel(groups, meta, *refs):
+    stored, (resumed_ref, restored_ref) = refs[:groups], refs[-2:]
     for s in range(SEQS):
         slot = meta.home(meta.group * SEQS + s)
         source = (slot // SEQS - meta.group + groups) % groups
@@ -264,6 +256,14 @@
         for j in range(1, groups):
             kept = jnp.where(source == j, stored[j][slot % SEQS], kept)
         restored_ref[s] = kept
+    for chip in range(resumed_ref.shape[0]):
+        closing = meta.session_at((chip + 1) * 2 * TOK - 1)
+        resumed_ref[chip] = restored_ref[closing].astype(jnp.bfloat16)
+
+
+def recurrence_kernel(local, meta, got_ref, restored_ref, *refs):
+    out_ref, token_ref = refs[-2:]
+    token_ref[...] = jnp.zeros_like(token_ref)
     width = local * N
     span = 2 * TOK
     state = [jnp.zeros((N, P_SIZE), jnp.float32) for _ in range(local)]
@@ -278,40 +278,8 @@
             rows = slice(k * N, (k + 1) * N)
             entering = jnp.where(opens, restored_ref[opening, rows, :], state[k])
             out_ref[c, rows, :] = entering.astype(jnp.bfloat16)
-            resumed = restored_ref[closing, rows, :]
-            out_ref[c, width + k * N : width + (k + 1) * N, :] = resumed.astype(jnp.bfloat16)
-            source = jnp.where(closes, resumed, state[k])
+            source = jnp.where(closes, restored_ref[closing, rows, :], state[k])
             state[k] = factor[k : k + 1] * source + got_ref[c, rows, :].astype(jnp.float32)
-
-
-def middle_kernel(local, meta, entering_ref, keep_ref, got_ref, *refs):
-    even = meta.even
-    first = meta.place // 2 * 2 * TOK
-    second = first + TOK
-    start = meta.start_of(meta.session_at(second + TOK - 1))
-    closes = (start > first) & (start < second)
-    opens = start == second
-    width = local * N
-    own_ref, send_ref = refs[-2:]
-    for chip in range(entering_ref.shape[0]):
-        f0 = jnp.where(
-            even,
-            factors_of(keep_ref[chip, width:, :], local),
-            factors_of(got_ref[chip, width:, :], local),
-        )
-        resumed = entering_ref[chip, width:, :].astype(jnp.float32)
-        own_ref[chip, width:, :] = entering_ref[chip, width:, :]
-        send_ref[chip, width:, :] = entering_ref[chip, width:, :]
-        for k in range(local):
-            rows = slice(k * N, (k + 1) * N)
-            entering = entering_ref[chip, rows, :].astype(jnp.float32)
-            s0 = jnp.where(
-                even, keep_ref[chip, rows, :].astype(jnp.float32), got_ref[chip, rows, :].astype(jnp.float32)
-            )
-            middle = f0[k : k + 1] * jnp.where(closes, resumed[rows], entering) + s0
-            middle = jnp.where(opens, resumed[rows], middle)
-            own_ref[chip, rows, :] = jnp.where(even, entering, middle).astype(jnp.bfloat16)
-            send_ref[chip, rows, :] = jnp.where(even, middle, entering).astype(jnp.bfloat16)
 
 
 def intra_kernel(meta, skip, x_ref, dl_ref, step_ref, write_ref, read_ref, _, out_ref, token_ref, run_s, step_s):
@@ -380,11 +348,18 @@
 
 
 def finish_kernel(
-    local, meta, part_ref, dl_ref, step_ref, read_ref, own_ref, other_ref, out_ref, factor_s
+    local, meta, part_ref, dl_ref, read_ref, own_ref, other_ref, mine_ref, theirs_ref, low_ref, high_ref, _, out_ref,
+    factor_s,
 ):
     step = pl.program_id(0)
     even = meta.even
     r = meta.last_start()
+    first = meta.place // 2 * 2 * TOK
+    second = first + TOK
+    start = meta.start_of(meta.session_at(second + TOK - 1))
+    closes = (start > first) & (start < second)
+    opens = start == second
+    width = local * N
 
     @pl.when(step == 0)
     def _():
@@ -396,32 +371,33 @@
     factor = factor_s[pl.ds(pl.multiple_of(step * PAIR, PAIR), PAIR), :].T
     token = lax.broadcasted_iota(jnp.int32, (TOK, N), 0)
     resumed = (token >= r) & (r > 0)
+    decays = [[factors_of(ref[chip, width:, :], local) for ref in (low_ref, high_ref)] for chip in range(own_ref.shape[0])]
     for group in range(2):
         reads = read_ref[:, group * N : (group + 1) * N].astype(jnp.float32)
         left = jnp.where(resumed, 0.0, reads)
         right = jnp.where(resumed, reads, 0.0)
         reads = jnp.concatenate([left, right], axis=1).astype(jnp.bfloat16)
         for k in range(group * HEADS_PER, (group + 1) * HEADS_PER):
-            chip, half = k // (2 * local), k // local % 2
-            rows = slice((k % local) * N, (k % local + 1) * N)
+            chip, half, head = k // (2 * local), k // local % 2, k % local
+            rows = slice(head * N, (head + 1) * N)
             own = even if half == 0 else jnp.logical_not(even)
-            later = slice(rows.start + local * N, rows.stop + local * N)
-            states = jnp.concatenate(
-                [
-                    jnp.where(own, own_ref[chip, rows, :], other_ref[chip, rows, :]),
-                    jnp.where(own, own_ref[chip, later, :], other_ref[chip, later, :]),
-                ],
-                axis=0,
-            )
+            entering = jnp.where(own, own_ref[chip, rows, :], other_ref[chip, rows, :]).astype(jnp.float32)
+            restored = jnp.where(own, mine_ref[chip, rows, :], theirs_ref[chip, rows, :])
+            whole_state = restored.astype(jnp.float32)
+            summary = (low_ref, high_ref)[half][chip, rows, :].astype(jnp.float32)
+            middle = decays[chip][half][head : head + 1] * jnp.where(closes, whole_state, entering) + summary
+            middle = jnp.where(opens, whole_state, middle)
+            entering = jnp.where(even, entering, middle).astype(jnp.bfloat16)
+            states = jnp.concatenate([entering, restored], axis=0)
             carried = jnp.dot(reads, states, preferred_element_type=jnp.float32)
             place = slice(k * P_SIZE, (k + 1) * P_SIZE)
             out_ref[:, place] = (part_ref[:, place] + factor[:, k : k + 1] * carried).astype(jnp.bfloat16)
 
 
-def finish(meta, part, rates, steps, reads, own, other, local):
+def finish(meta, part, rates, reads, own, other, mine, theirs, low, high, local, idle):
     chips = PAIR // (2 * local)
-    width = 2 * local * N
-    states = pl.BlockSpec((chips, width, P_SIZE), lambda i, *m: (i, 0, 0))
+    states = pl.BlockSpec((chips, local * N, P_SIZE), lambda i, *m: (i, 0, 0))
+    stretch = pl.BlockSpec((chips, local * N + EXTRA, P_SIZE), lambda i, *m: (i, 0, 0))
     return pl.pallas_call(
         scalars(finish_kernel, local),
         out_shape=jax.ShapeDtypeStruct((TOK, H * P_SIZE), jnp.bfloat16),
@@ -431,10 +407,14 @@
             in_specs=[
                 pl.BlockSpec((TOK, PAIR * P_SIZE), lambda i, *m: (0, i)),
                 pl.BlockSpec((H, TOK), lambda i, *m: (0, 0)),
-                pl.BlockSpec((H, TOK), lambda i, *m: (0, 0)),
                 pl.BlockSpec((TOK, 2 * N), lambda i, *m: (0, i)),
                 states,
                 states,
+                states,
+                states,
+                stretch,
+                stretch,
+                idle_spec(idle),
             ],
             out_specs=pl.BlockSpec((TOK, PAIR * P_SIZE), lambda i, *m: (0, i)),
             scratch_shapes=[pltpu.VMEM((H, TOK), jnp.float32)],
@@ -442,11 +422,11 @@
         compiler_params=params(),
         cost_estimate=LONG,
         name="finish",
-    )(meta, part, rates, steps, reads, own, other)
+    )(meta, part, rates, reads, own, other, mine, theirs, low, high, idle)
 
 
 def attend_kernel(
-    meta, q_ref, band4, band3, band2, band1, band0, *refs,
+    meta, q_ref, four, two, now, four_across, two_across, now_across, *refs,
 ):
     history_refs, (sk_ref, sv_ref), (out_ref, token_ref, key_s, value_s) = refs[:16], refs[16:18], refs[-4:]
     factor = 1.0 / math.sqrt(HD)
@@ -454,7 +434,19 @@
     r = meta.last_start()
     opening = meta.session_at(first)
     closing = meta.session_at(first + TOK - 1)
-    bands = (band4, band3.at[0], band2, band1.at[0], band0)
+    even = meta.even
+
+    def band(number, part):
+        if number == 0:
+            return four[part]
+        if number == 1:
+            return jnp.where(even, four_across[part], two_across[part])
+        if number == 2:
+            return two[part]
+        if number == 3:
+            return jnp.where(even, two_across[part], now_across[part])
+        return now[part]
+
     token_ref[...] = jnp.zeros_like(token_ref)
 
     def sinks(ref, session):
@@ -485,23 +477,23 @@
             history = jnp.dot(
                 moved, jnp.concatenate([keys, values], axis=1), preferred_element_type=jnp.float32
             )
-            for i, band in enumerate(bands):
+            for i in range(REACH + 1):
                 rows = slice(i * TOK, (i + 1) * TOK)
                 index = lax.broadcasted_iota(jnp.int32, (TOK, HD), 0) + i * TOK
                 turn = index >= start
                 key_s[rows, :] = jnp.where(
-                    turn, band[0].astype(jnp.float32), history[rows, :HD]
+                    turn, band(i, 0).astype(jnp.float32), history[rows, :HD]
                 ).astype(jnp.bfloat16)
                 value_s[rows, :] = jnp.where(
-                    turn, band[1].astype(jnp.float32), history[rows, HD:]
+                    turn, band(i, 1).astype(jnp.float32), history[rows, HD:]
                 ).astype(jnp.bfloat16)
 
         @pl.when(needed & (start <= 0))
         def _():
-            for i, band in enumerate(bands):
+            for i in range(REACH + 1):
                 rows = slice(i * TOK, (i + 1) * TOK)
-                key_s[rows, :] = band[0]
-                value_s[rows, :] = band[1]
+                key_s[rows, :] = band(i, 0)
+                value_s[rows, :] = band(i, 1)
 
         for b in range(TOK // BLOCK):
             inside = (b * BLOCK + BLOCK > r) if resuming else (b * BLOCK < r)
@@ -559,11 +551,6 @@
 
         return pl.BlockSpec((chips, share, HD), index)
 
-    def band_spec(array, number):
-        if array.ndim == 3:
-            return pl.BlockSpec((2, TOK, HD), lambda j, *m: (0, 0, j))
-        return pl.BlockSpec((1, 2, TOK, HD), lambda j, *m: (number, 0, 0, j))
-
     pad = SEQS, SINKS, HD
     return pl.pallas_call(
         scalars(attend_kernel),
@@ -572,7 +559,7 @@
             num_scalar_prefetch=1,
             grid=(KVH,),
             in_specs=[pl.BlockSpec((TOK, lanes), lambda j, *m: (0, j))]
-            + [band_spec(a, number) for a, number in zip(bands, (0, 1, 0, 0, 0))]
+            + [pl.BlockSpec((2, TOK, HD), lambda j, *m: (0, 0, j))] * len(bands)
             + [history_spec(0, False)] * 4
             + [history_spec(1, False)] * 4
             + [history_spec(0, True)] * 4
@@ -647,6 +634,7 @@
         meta,
         [cache_keys[0], cache_values[0], turn_keys[0], turn_values[0]],
         [(parcel, jnp.bfloat16), (parcel, jnp.bfloat16), (band, jnp.bfloat16)],
+        mib=60,
     )
     distance = devices // 2
     moved = apart(away, distance)
@@ -691,45 +679,43 @@
         idle=[turned, two],
     )
     total = exchanged(chip)
-    [pair] = whole(
-        scalars(pair_kernel), "pair", meta, [key_value, two, four], [((2, *band), jnp.bfloat16)], idle=[chip]
-    )
-    after = pair
-    pair = apart(pair, 1)
+    after = chip
     while distance > 2:
         [near] = whole(scalars(join_kernel), "join", meta, [near, moved], [joined(near)], idle=[after])
         after = near
         distance //= 2
         moved = apart(near, distance)
     beside = moved
-    across = apart(near, 1)
-    part, token = intra(meta, skip_gain, x, rates, steps, writes, reads, after)
+    resumed, restored = whole(
+        scalars(restore_kernel, groups),
+        "restore",
+        meta,
+        stored,
+        [((chips, width, P_SIZE), jnp.bfloat16), ((SEQS, width, P_SIZE), jnp.float32)],
+        idle=[after],
+    )
+    mine = exchanged(resumed)
+    part, token = intra(meta, skip_gain, x, rates, steps, writes, reads, restored)
 
     entering, after = whole(
-        scalars(recurrence_kernel, local, groups),
+        scalars(recurrence_kernel, local),
         "recurrence",
         meta,
-        [total, *stored],
-        [((chips, 2 * width, P_SIZE), jnp.bfloat16), (TOKEN.shape, TOKEN.dtype)],
-        idle=[token, beside, across, pair],
-        scratch=[pltpu.VMEM((SEQS, width, P_SIZE), jnp.float32)],
+        [total, restored],
+        [((chips, width, P_SIZE), jnp.bfloat16), (TOKEN.shape, TOKEN.dtype)],
+        idle=[token, beside, mine],
     )
     entering = exchanged(entering)
-    pieces = [near, beside, across, apart(beside, 1)]
-    bands = [four, pair, two, pair, key_value]
+    pieces = [near, beside, apart(near, 1), apart(beside, 1)]
+    bands = [four, two, key_value]
+    bands += [apart(block, 1) for block in bands]
+    theirs = apart(mine, 1)
+    low = apart(keep, 1)
     attended, token = attend(
-        meta, queries[0], bands, pieces, devices // 2, sink_keys[0], sink_values[0], [after]
-    )
-    own, other = whole(
-        scalars(middle_kernel, local),
-        "middle",
-        meta,
-        [entering, keep, got],
-        [((chips, 2 * width, P_SIZE), jnp.bfloat16)] * 2,
-        idle=[token],
-    )
-    other = apart(other, 1)
-    mixed = finish(meta, part, rates, steps, reads, own, other, local)
+        meta, queries[0], bands, pieces, devices // 2, sink_keys[0], sink_values[0], [after, theirs, low]
+    )
+    other = apart(entering, 1)
+    mixed = finish(meta, part, rates, reads, entering, other, mine, theirs, low, got, local, token)
     return mixed[None], attended[None]
 
 

time: 121 us -> 123 us (1.017); the launches traced: 120 us -> 123 us
  Pallas kernels: 55.1 us -> 46.9 us
  starting transfers between devices: 27.1 us -> 34.6 us
  waiting for transfers between devices: 27.6 us -> 34.5 us
  local copies, waits for them, and re-layouts: 9.14 us -> 6.46 us
    all_to_all x2 -> x3, waiting for transfers between devices: 12 us -> 26.3 us  [exchanged(): lax.all_to_all(block, 'ctx', 0, 0, axis_index_groups=same_core, tiled=True)]
    pallas_call x8 -> x7, Pallas kernels: 23.3 us -> 9.11 us  [whole(): pl.pallas_call(kernel, out_shape=[jax.ShapeDtypeStruct(s, t) for s, t in...]
    ppermute x9 -> x13, waiting for transfers between devices: 15.7 us -> 8.19 us  [apart(): lax.ppermute(block, 'ctx', [(i, i ^ distance) for i in range(devices)])]
    all_to_all x2 -> x3, starting transfers between devices: 10 us -> 16.4 us  [exchanged(): lax.all_to_all(block, 'ctx', 0, 0, axis_index_groups=same_core, tiled=True)]
    pallas_call x1, Pallas kernels: 13.4 us -> 18.7 us  [attend(): pl.pallas_call(scalars(attend_kernel), out_shape=[jax.ShapeDtypeStruct((T...]
    unnamed x34 -> x46, local copies, waits for them, and re-layouts: 6.56 us -> 4.7 us
    ppermute x9 -> x13, starting transfers between devices: 11.1 us -> 12.2 us  [apart(): lax.ppermute(block, 'ctx', [(i, i ^ distance) for i in range(devices)])]
  transfers between devices with their start and end apart: 13 -> 18, of which waited for: 5 -> 6; matrix products, arithmetic and copies ran while one was open for 1% -> 0% of each run, Pallas kernels for 29% -> 24%
where the time goes in v2:
time: 123 us
  Pallas kernels  46.9 us (38%)
  starting transfers between devices  34.6 us (28%)
  waiting for transfers between devices  34.5 us (28%)
  local copies, waits for them, and re-layouts  6.46 us (5%)
    all_to_all x3, waiting for transfers between devices, exchanged(): lax.all_to_all(block, 'ctx', 0, 0, axis_index_groups=same_core, tiled=True)  26.3 us
    pallas_call x1, Pallas kernels, attend(): pl.pallas_call(scalars(attend_kernel), out_shape=[jax.ShapeDtypeStruct((T...  18.7 us
    all_to_all x3, starting transfers between devices, exchanged(): lax.all_to_all(block, 'ctx', 0, 0, axis_index_groups=same_core, tiled=True)  16.4 us
    ppermute x13, starting transfers between devices, apart(): lax.ppermute(block, 'ctx', [(i, i ^ distance) for i in range(devices)])  12.2 us
    pallas_call x7, Pallas kernels, whole(): pl.pallas_call(kernel, out_shape=[jax.ShapeDtypeStruct(s, t) for s, t in...  9.11 us
    ppermute x13, waiting for transfers between devices, apart(): lax.ppermute(block, 'ctx', [(i, i ^ distance) for i in range(devices)])  8.19 us
    pallas_call x1, Pallas kernels, finish(): pl.pallas_call(scalars(finish_kernel, local), out_shape=jax.ShapeDtypeStr...  7.18 us
    pallas_call x1, Pallas kernels, intra(): pl.pallas_call(scalars(intra_kernel), out_shape=[jax.ShapeDtypeStruct((TO...  6.66 us
  transfers between devices with their start and end apart: 18, of which 6 were waited for; matrix products, arithmetic and copies ran while one was open for 0% of the time, Pallas kernels for 24%

profile of v2, /device:TPU:0, one launch (start us, length us, event | category | flops | bytes accessed | tf_op | source)
XLA Modules:
  0.0 123.3 jit_solution(10427835779876805661)
XLA Ops:
  0.6 1.3 %concatenate.3.ids = s32[14]{0:T(128)} concatenate(s32[1]{0:T(128)} %bitcast, s32[1]{0:T(128)} %bitcast.1, s32[3]{0:T(128)} %bitcast.22, s32[3]{0:T(128)} %bitcast.23, s32[6]{0:T(128)} %param.24), dimensions={0} | concatenate | bytes 112 | tf_op jit(solution)/shard_map/concatenate | solution.py:618
  2.0 2.6 %pack.1 = (bf16[1,512,128]{2,1,0:T(8,128)(2,1)}, bf16[1,512,128]{2,1,0:T(8,128)(2,1)}, bf16[2,128,512]{2,1,0:T(8,128)(2,1)}) custom-call(s32[14]{0:T(128)} %concatenate.3.ids, bf16[3,32,512]{2,1,0:T(8,128)(2,1)} %bitcast.33, bf16[3,32,512]{2,1,0:T(8,128)(2,1)} %bitcast.34, bf16[128,512]{1,0:T(8,128)(2,1)} %bitcast.27, bf16[128,512]{1,0:T(8,128)(2,1)} %bitcast.28), custom_call_target="tpu_custom_call" | custom-call | flops 34359738368 | bytes 1048576 | tf_op jit(solution)/shard_map/pack/pallas_call | solution.py:172
  4.6 0.0 copy-start.1
  4.6 0.0 copy-start.14
  4.6 5.2 %summaries.1 = (bf16[8,272,128]{2,1,0:T(8,128)(2,1)}, bf16[8,272,128]{2,1,0:T(8,128)(2,1)}) custom-call(s32[14]{0:T(128)} %concatenate.3.ids, bf16[128,8192]{1,0:T(8,128)(2,1)} %bitcast.24, bf16[64,128]{1,0:T(8,128)(2,1)} %bitcast.37, bf16[64,128]{1,0:T(8,128)(2,1)} %bitcast.35, bf16[128,512]{1,0:T(8,128)(2,1)} %bitcast.29, ...), custom_call_target="tpu_custom_call" | custom-call | flops 34359738368 | bytes 1048576 | tf_op jit(solution)/shard_map/summaries/pallas_call | solution.py:138
  9.8 0.4 collective-permute-start.2
  10.3 0.0 copy-done.7
  10.3 4.5 %collective-permute-start.1 = (bf16[2,128,512]{2,1,0:T(8,128)(2,1)S(1)}, bf16[2,128,512]{2,1,0:T(8,128)(2,1)S(1)}, u32[]{:S(2)}, u32[]{:S(2)}) collective-permute-start(bf16[2,128,512]{2,1,0:T(8,128)(2,1)S(1)} %copy-done.7), channel_id=1, source_target_pairs={{0,4},{1,5},{2,6},{3,7},{4,8},{5,9},{6,10},{7,11},{8,12},{9,13},{1... | collective-permute-start | bytes 786440 | tf_op jit(solution)/shard_map/ppermute | solution.py:588
  14.8 2.6 %collective-permute-start = (bf16[1,512,128]{2,1,0:T(8,128)(2,1)S(1)}, bf16[1,512,128]{2,1,0:T(8,128)(2,1)S(1)}, u32[]{:S(2)}, u32[]{:S(2)}) collective-permute-start(bf16[1,512,128]{2,1,0:T(8,128)(2,1)S(1)} %copy-done.22), channel_id=1, source_target_pairs={{0,8},{1,9},{2,10},{3,11},{4,12},{5,13},{6,14},{7,15},{8,0},{9,1},... | collective-permute-start | bytes 393224 | tf_op jit(solution)/shard_map/ppermute | solution.py:624
  17.4 0.4 reshape_squeeze.3.refs_0_
  17.8 6.3 %collective-permute-done.refs_1_ = bf16[1,512,128]{2,1,0:T(8,128)(2,1)S(1)} collective-permute-done((bf16[1,512,128]{2,1,0:T(8,128)(2,1)S(1)}, bf16[1,512,128]{2,1,0:T(8,128)(2,1)S(1)}, u32[]{:S(2)}, u32[]{:S(2)}) %collective-permute-start) | collective-permute-done | bytes 131104 | tf_op jit(solution)/shard_map/ppermute | solution.py:624
  24.2 0.0 collective-permute-done.1.refs_3_.refs_1_
  24.2 0.0 collective-permute-done.2.refs_4_.refs_1_.refs_8_
  24.2 0.6 join_two.1
  24.8 0.1 copy-done.9
  24.9 1.5 %collective-permute-start.5 = (bf16[2,128,512]{2,1,0:T(8,128)(2,1)S(1)}, bf16[2,128,512]{2,1,0:T(8,128)(2,1)S(1)}, u32[]{:S(2)}, u32[]{:S(2)}) collective-permute-start(bf16[2,128,512]{2,1,0:T(8,128)(2,1)S(1)} %get-tuple-element.21.refs_1_), channel_id=1, source_target_pairs={{0,2},{1,3},{2,0},{3,1},{4,6},{5,7},{6,4},{7,5},{8,10},{9,11},{10,... | collective-permute-start | bytes 786440 | tf_op jit(solution)/shard_map/ppermute | solution.py:624
  26.4 0.8 turn.1.refs_2_.refs_0_
  27.2 4.0 %collective-permute-start.4 = (bf16[2,512,128]{2,1,0:T(8,128)(2,1)S(1)}, bf16[2,512,128]{2,1,0:T(8,128)(2,1)S(1)}, u32[]{:S(2)}, u32[]{:S(2)}) collective-permute-start(bf16[2,512,128]{2,1,0:T(8,128)(2,1)S(1)} %get-tuple-element.22.refs_0_), channel_id=1, source_target_pairs={{0,4},{1,5},{2,6},{3,7},{4,0},{5,1},{6,2},{7,3},{8,12},{9,13},{10,... | collective-permute-start | bytes 786440 | tf_op jit(solution)/shard_map/ppermute | solution.py:624
  31.3 1.5 %collective-permute-start.3 = (f32[3,256,128]{2,1,0:T(8,128)S(1)}, f32[3,256,128]{2,1,0:T(8,128)S(1)}, u32[]{:S(2)}, u32[]{:S(2)}) collective-permute-start(f32[3,256,128]{2,1,0:T(8,128)S(1)} %turn.1.refs_2_.refs_0_), channel_id=1, source_target_pairs={{16,0},{0,16},{17,1},{1,17},{18,2},{2,18},{19,3},{3,19},{20,4},{4,... | collective-permute-start | bytes 1179656 | tf_op jit(solution)/shard_map/ppermute | solution.py:671
  32.8 0.0 collective-permute-done.5.refs_3_.refs_2_
  32.8 1.6 %combine.1.refs_2_ = bf16[8,272,128]{2,1,0:T(8,128)(2,1)} custom-call(s32[14]{0:T(128)S(1)} %copy-done.1, bf16[8,272,128]{2,1,0:T(8,128)(2,1)S(1)} %copy-done.4, bf16[8,272,128]{2,1,0:T(8,128)(2,1)S(1)} %collective-permute-done.2.refs_4_.refs_1_.refs_8_, f32[3,256,128]{2,1,0:T(8,128)S(1)} %turn.1.refs_2_.refs_0_, ...), custom_call_target="tpu_custom_call" | custom-call | flops 34359738368 | bytes 1048576 | tf_op jit(solution)/shard_map/combine/pallas_call | solution.py:172
  34.4 9.1 %all-to-all-start = ((bf16[8,272,128]{2,1,0:T(8,128)(2,1)}), bf16[8,272,128]{2,1,0:T(8,128)(2,1)S(1)}, u32[]{:S(2)}, u32[]{:S(2)}) async-start(bf16[8,272,128]{2,1,0:T(8,128)(2,1)} %combine.1.refs_2_), calls=%async_computation | async-start | bytes 1114112 | tf_op jit(solution)/shard_map/all_to_all | solution.py:627
  43.5 0.0 collective-permute-done.4.refs_1_
  43.5 0.6 join.1.refs_2_.refs_7_.refs_11_.refs_15_.refs_19_
  44.1 2.1 %collective-permute-start.6 = (bf16[4,512,128]{2,1,0:T(8,128)(2,1)S(1)}, bf16[4,512,128]{2,1,0:T(8,128)(2,1)S(1)}, u32[]{:S(2)}, u32[]{:S(2)}) collective-permute-start(bf16[4,512,128]{2,1,0:T(8,128)(2,1)S(1)} %join.1.refs_2_.refs_7_.refs_11_.refs_15_.refs_19_), channel_id=1, source_target_pairs={{0,2},{1,3},{2,0},{3,1},{4,6},{5,7},{6,4},{7,5},{8,10},{9,11},{10,... | collective-permute-start | bytes 1572872 | tf_op jit(solution)/shard_map/ppermute | solution.py:624
  46.2 0.0 collective-permute-done.3.refs_1_
  46.2 1.5 %restore.1 = (bf16[8,256,128]{2,1,0:T(8,128)(2,1)}, f32[3,256,128]{2,1,0:T(8,128)S(1)}) custom-call(s32[14]{0:T(128)S(1)} %copy-done.1, f32[3,256,128]{2,1,0:T(8,128)S(1)} %turn.1.refs_2_.refs_0_, f32[3,256,128]{2,1,0:T(8,128)S(1)} %collective-permute-done.3.refs_1_, bf16[4,512,128]{2,1,0:T(8,128)(2,1)S(1)} %join.1.refs_2_.refs_7_.refs_11_.refs_15_.refs_19_), custom_call_target="tpu_custom_call" | custom-call | flops 34359738368 | bytes 1048576 | tf_op jit(solution)/shard_map/restore/pallas_call | solution.py:172
  47.6 0.8 copy-done.12
  48.4 9.3 %all-to-all-done.refs_0_ = bf16[8,272,128]{2,1,0:T(8,128)(2,1)S(1)} async-done(((bf16[8,272,128]{2,1,0:T(8,128)(2,1)}), bf16[8,272,128]{2,1,0:T(8,128)(2,1)S(1)}, u32[]{:S(2)}, u32[]{:S(2)}) %all-to-all-start) | async-done | bytes 557088 | tf_op jit(solution)/shard_map/all_to_all | solution.py:627
  57.7 3.7 %all-to-all-start.1 = ((bf16[8,256,128]{2,1,0:T(8,128)(2,1)}), bf16[8,256,128]{2,1,0:T(8,128)(2,1)S(1)}, u32[]{:S(2)}, u32[]{:S(2)}) async-start(bf16[8,256,128]{2,1,0:T(8,128)(2,1)} %get-tuple-element.27), calls=%async_computation.1 | async-start | bytes 1048576 | tf_op jit(solution)/shard_map/all_to_all | solution.py:627
  61.4 6.7 %intra.1 = (f32[128,8192]{1,0:T(8,128)}, f32[8,128]{1,0:T(8,128)}) custom-call(s32[14]{0:T(128)} %concatenate.3.ids, f32[64]{0:T(128)} %refs_0_.1, bf16[128,8192]{1,0:T(8,128)(2,1)} %bitcast.25, bf16[64,128]{1,0:T(8,128)(2,1)} %bitcast.38, bf16[64,128]{1,0:T(8,128)(2,1)} %bitcast.36, bf16[128,512]{1,0:T(8,128)(2,1)} %bitcast.30, bf16[128,512]{1,0:T(8,128)(2,1)} %bitcast.31, ...), custom_call_target="tpu_custom_call" | custom-call | flops 34359738368 | bytes 1048576 | tf_op jit(solution)/shard_map/intra/pallas_call | solution.py:321
  68.0 0.0 collective-permute-done.6.refs_3_.refs_8_.refs_12_.refs_16_.refs_20_
  68.0 7.1 %all-to-all-done.1.refs_4_.refs_5_ = bf16[8,256,128]{2,1,0:T(8,128)(2,1)S(1)} async-done(((bf16[8,256,128]{2,1,0:T(8,128)(2,1)}), bf16[8,256,128]{2,1,0:T(8,128)(2,1)S(1)}, u32[]{:S(2)}, u32[]{:S(2)}) %all-to-all-start.1) | async-done | bytes 524320 | tf_op jit(solution)/shard_map/all_to_all | solution.py:627
  75.1 0.0 copy-done.2
  75.1 1.2 copy-done.13
  76.3 0.7 copy-done.16
  77.0 1.5 %recurrence.1 = (bf16[8,256,128]{2,1,0:T(8,128)(2,1)}, f32[8,128]{1,0:T(8,128)S(1)}) custom-call(s32[14]{0:T(128)S(1)} %copy-done.2, bf16[8,272,128]{2,1,0:T(8,128)(2,1)S(1)} %all-to-all-done.refs_0_, f32[3,256,128]{2,1,0:T(8,128)S(1)} %copy-done.13, f32[8,128]{1,0:T(8,128)S(1)} %copy-done.16, ...), custom_call_target="tpu_custom_call" | custom-call | flops 34359738368 | bytes 1048576 | tf_op jit(solution)/shard_map/recurrence/pallas_call | solution.py:172
  78.5 0.6 copy-done.15
  79.1 3.6 %all-to-all-start.2 = ((bf16[8,256,128]{2,1,0:T(8,128)(2,1)}), bf16[8,256,128]{2,1,0:T(8,128)(2,1)S(1)}, u32[]{:S(2)}, u32[]{:S(2)}) async-start(bf16[8,256,128]{2,1,0:T(8,128)(2,1)} %get-tuple-element.28), calls=%async_computation.2 | async-start | bytes 1048576 | tf_op jit(solution)/shard_map/all_to_all | solution.py:627
  82.7 0.0 copy-done.8
  82.7 0.1 collective-permute-start.12
  82.8 0.5 collective-permute-start.9
  83.3 0.0 copy-done.10
  83.3 0.1 collective-permute-start.10
  83.4 0.4 collective-permute-start.13
  83.8 0.1 collective-permute-start.14
  83.9 0.4 collective-permute-done.12.refs_6_
  84.3 0.0 copy-done
  84.3 0.1 collective-permute-start.8
  84.5 1.4 %collective-permute-done.10.refs_4_ = bf16[2,128,512]{2,1,0:T(8,128)(2,1)S(1)} collective-permute-done((bf16[2,128,512]{2,1,0:T(8,128)(2,1)S(1)}, bf16[2,128,512]{2,1,0:T(8,128)(2,1)S(1)}, u32[]{:S(2)}, u32[]{:S(2)}) %collective-permute-start.10) | collective-permute-done | bytes 262176 | tf_op jit(solution)/shard_map/ppermute | solution.py:624
  85.9 0.1 collective-permute-start.11
  86.0 0.6 copy-done.21
  86.6 0.0 collective-permute-done.9.refs_27_.refs_7_
  86.6 9.9 %all-to-all-done.2.refs_3_ = bf16[8,256,128]{2,1,0:T(8,128)(2,1)S(1)} async-done(((bf16[8,256,128]{2,1,0:T(8,128)(2,1)}), bf16[8,256,128]{2,1,0:T(8,128)(2,1)S(1)}, u32[]{:S(2)}, u32[]{:S(2)}) %all-to-all-start.2) | async-done | bytes 524320 | tf_op jit(solution)/shard_map/all_to_all | solution.py:627
  96.5 0.0 collective-permute-start.7
  96.5 0.0 collective-permute-done.11.refs_5_
  96.5 0.0 collective-permute-done.13.refs_9_.refs_13_.refs_17_.refs_21_
  96.5 0.0 collective-permute-done.14.refs_10_.refs_14_.refs_18_.refs_22_
  96.5 0.0 collective-permute-done.8.refs_26_.refs_6_
  96.6 18.7 %attend.1 = (bf16[128,4096]{1,0:T(8,128)(2,1)}, f32[8,128]{1,0:T(8,128)}) custom-call(s32[14]{0:T(128)} %concatenate.3.ids, bf16[128,4096]{1,0:T(8,128)(2,1)} %bitcast.26, bf16[2,128,512]{2,1,0:T(8,128)(2,1)} %copy-done.9, bf16[2,128,512]{2,1,0:T(8,128)(2,1)} %copy-done.11, bf16[2,128,512]{2,1,0:T(8,128)(2,1)} %get-tuple-element.19.refs_2_.refs_3_, ...), custom_call_target="tpu_custom_call" | custom-call | flops 34359738368 | bytes 1048576 | tf_op jit(solution)/shard_map/attend/pallas_call | solution.py:555
  115.3 0.0 copy-done.17
  115.3 0.0 collective-permute-done.7.refs_4_
  115.3 0.8 copy-done.19
  116.1 7.2 %finish.1 = bf16[128,8192]{1,0:T(8,128)(2,1)} custom-call(s32[14]{0:T(128)} %concatenate.3.ids, f32[128,8192]{1,0:T(8,128)} %get-tuple-element.25.refs_0_, bf16[64,128]{1,0:T(8,128)(2,1)} %bitcast.39, bf16[128,512]{1,0:T(8,128)(2,1)} %bitcast.32, bf16[8,256,128]{2,1,0:T(8,128)(2,1)} %copy-done.17, bf16[8,256,128]{2,1,0:T(8,128)(2,1)} %copy-done.19, ...), custom_call_target="tpu_custom_call" | custom-call | flops 34359738368 | bytes 1048576 | tf_op jit(solution)/shard_map/finish/pallas_call | solution.py:401
  (31 shorter events, 0.1 us)
Async XLA Ops:
  4.5 5.7 %copy-start.7 = (bf16[2,128,512]{2,1,0:T(8,128)(2,1)S(1)}, bf16[2,128,512]{2,1,0:T(8,128)(2,1)}, u32[]{:S(2)}) copy-start(bf16[2,128,512]{2,1,0:T(8,128)(2,1)} %get-tuple-element.19.refs_2_.refs_3_) | copy-start | bytes 786436
  4.5 10.2 %copy-start.22 = (bf16[1,512,128]{2,1,0:T(8,128)(2,1)S(1)}, bf16[1,512,128]{2,1,0:T(8,128)(2,1)}, u32[]{:S(2)}) copy-start(bf16[1,512,128]{2,1,0:T(8,128)(2,1)} %get-tuple-element.18.refs_4_) | copy-start | bytes 393220
  4.5 12.9 %copy-start.18 = (f32[1,3,4,8192]{3,2,1,0:T(4,128)S(1)}, f32[1,3,4,8192]{3,2,1,0:T(4,128)}, u32[]{:S(2)}) copy-start(f32[1,3,4,8192]{3,2,1,0:T(4,128)} %param.23) | copy-start | bytes 1179652
  4.6 19.7 %copy-start.1 = (s32[14]{0:T(128)S(1)}, s32[14]{0:T(128)}, u32[]{:S(2)}) copy-start(s32[14]{0:T(128)} %concatenate.3.ids) | copy-start | bytes 172
  4.6 19.7 %copy-start.14 = (bf16[1,512,128]{2,1,0:T(8,128)(2,1)S(1)}, bf16[1,512,128]{2,1,0:T(8,128)(2,1)}, u32[]{:S(2)}) copy-start(bf16[1,512,128]{2,1,0:T(8,128)(2,1)} %get-tuple-element.17.refs_0_) | copy-start | bytes 393220
  9.8 14.4 %collective-permute-start.2 = (bf16[8,272,128]{2,1,0:T(8,128)(2,1)}, bf16[8,272,128]{2,1,0:T(8,128)(2,1)S(1)}, u32[]{:S(2)}, u32[]{:S(2)}) collective-permute-start(bf16[8,272,128]{2,1,0:T(8,128)(2,1)} %get-tuple-element.20), channel_id=1, source_target_pairs={{0,1},{1,0},{2,3},{3,2},{4,5},{5,4},{6,7},{7,6},{8,9},{9,8},{10,11... | collective-permute-start | bytes 1671176 | tf_op jit(solution)/shard_map/ppermute | solution.py:624
  10.3 13.9 %collective-permute-start.1 = (bf16[2,128,512]{2,1,0:T(8,128)(2,1)S(1)}, bf16[2,128,512]{2,1,0:T(8,128)(2,1)S(1)}, u32[]{:S(2)}, u32[]{:S(2)}) collective-permute-start(bf16[2,128,512]{2,1,0:T(8,128)(2,1)S(1)} %copy-done.7), channel_id=1, source_target_pairs={{0,4},{1,5},{2,6},{3,7},{4,8},{5,9},{6,10},{7,11},{8,12},{9,13},{1... | collective-permute-start | bytes 786440 | tf_op jit(solution)/shard_map/ppermute | solution.py:588
  14.8 9.4 %collective-permute-start = (bf16[1,512,128]{2,1,0:T(8,128)(2,1)S(1)}, bf16[1,512,128]{2,1,0:T(8,128)(2,1)S(1)}, u32[]{:S(2)}, u32[]{:S(2)}) collective-permute-start(bf16[1,512,128]{2,1,0:T(8,128)(2,1)S(1)} %copy-done.22), channel_id=1, source_target_pairs={{0,8},{1,9},{2,10},{3,11},{4,12},{5,13},{6,14},{7,15},{8,0},{9,1},... | collective-permute-start | bytes 393224 | tf_op jit(solution)/shard_map/ppermute | solution.py:624
  24.2 0.7 copy-start.9
  24.2 8.6 %copy-start.3 = (bf16[8,272,128]{2,1,0:T(8,128)(2,1)}, bf16[8,272,128]{2,1,0:T(8,128)(2,1)S(1)}, u32[]{:S(2)}) copy-start(bf16[8,272,128]{2,1,0:T(8,128)(2,1)S(1)} %collective-permute-done.2.refs_4_.refs_1_.refs_8_) | copy-start | bytes 1671172
  24.9 7.9 %copy-start.4 = (bf16[8,272,128]{2,1,0:T(8,128)(2,1)S(1)}, bf16[8,272,128]{2,1,0:T(8,128)(2,1)}, u32[]{:S(2)}) copy-start(bf16[8,272,128]{2,1,0:T(8,128)(2,1)} %get-tuple-element.23.refs_0_) | copy-start | bytes 1671172
  24.9 7.9 %collective-permute-start.5 = (bf16[2,128,512]{2,1,0:T(8,128)(2,1)S(1)}, bf16[2,128,512]{2,1,0:T(8,128)(2,1)S(1)}, u32[]{:S(2)}, u32[]{:S(2)}) collective-permute-start(bf16[2,128,512]{2,1,0:T(8,128)(2,1)S(1)} %get-tuple-element.21.refs_1_), channel_id=1, source_target_pairs={{0,2},{1,3},{2,0},{3,1},{4,6},{5,7},{6,4},{7,5},{8,10},{9,11},{10,... | collective-permute-start | bytes 786440 | tf_op jit(solution)/shard_map/ppermute | solution.py:624
  27.2 16.3 %collective-permute-start.4 = (bf16[2,512,128]{2,1,0:T(8,128)(2,1)S(1)}, bf16[2,512,128]{2,1,0:T(8,128)(2,1)S(1)}, u32[]{:S(2)}, u32[]{:S(2)}) collective-permute-start(bf16[2,512,128]{2,1,0:T(8,128)(2,1)S(1)} %get-tuple-element.22.refs_0_), channel_id=1, source_target_pairs={{0,4},{1,5},{2,6},{3,7},{4,0},{5,1},{6,2},{7,3},{8,12},{9,13},{10,... | collective-permute-start | bytes 786440 | tf_op jit(solution)/shard_map/ppermute | solution.py:624
  31.3 14.9 %collective-permute-start.3 = (f32[3,256,128]{2,1,0:T(8,128)S(1)}, f32[3,256,128]{2,1,0:T(8,128)S(1)}, u32[]{:S(2)}, u32[]{:S(2)}) collective-permute-start(f32[3,256,128]{2,1,0:T(8,128)S(1)} %turn.1.refs_2_.refs_0_), channel_id=1, source_target_pairs={{16,0},{0,16},{17,1},{1,17},{18,2},{2,18},{19,3},{3,19},{20,4},{4,... | collective-permute-start | bytes 1179656 | tf_op jit(solution)/shard_map/ppermute | solution.py:671
  32.8 53.1 %copy-start.11 = (bf16[2,128,512]{2,1,0:T(8,128)(2,1)}, bf16[2,128,512]{2,1,0:T(8,128)(2,1)S(1)}, u32[]{:S(2)}) copy-start(bf16[2,128,512]{2,1,0:T(8,128)(2,1)S(1)} %collective-permute-done.5.refs_3_.refs_2_) | copy-start | bytes 786436
  34.4 23.3 %all-to-all-start = ((bf16[8,272,128]{2,1,0:T(8,128)(2,1)}), bf16[8,272,128]{2,1,0:T(8,128)(2,1)S(1)}, u32[]{:S(2)}, u32[]{:S(2)}) async-start(bf16[8,272,128]{2,1,0:T(8,128)(2,1)} %combine.1.refs_2_), calls=%async_computation | async-start | bytes 1114112 | tf_op jit(solution)/shard_map/all_to_all | solution.py:627
  44.1 39.3 %copy-start.5 = (bf16[4,512,128]{2,1,0:T(8,128)(2,1)}, bf16[4,512,128]{2,1,0:T(8,128)(2,1)S(1)}, u32[]{:S(2)}) copy-start(bf16[4,512,128]{2,1,0:T(8,128)(2,1)S(1)} %join.1.refs_2_.refs_7_.refs_11_.refs_15_.refs_19_) | copy-start | bytes 1572868
  44.1 23.9 %collective-permute-start.6 = (bf16[4,512,128]{2,1,0:T(8,128)(2,1)S(1)}, bf16[4,512,128]{2,1,0:T(8,128)(2,1)S(1)}, u32[]{:S(2)}, u32[]{:S(2)}) collective-permute-start(bf16[4,512,128]{2,1,0:T(8,128)(2,1)S(1)} %join.1.refs_2_.refs_7_.refs_11_.refs_15_.refs_19_), channel_id=1, source_target_pairs={{0,2},{1,3},{2,0},{3,1},{4,6},{5,7},{6,4},{7,5},{8,10},{9,11},{10,... | collective-permute-start | bytes 1572872 | tf_op jit(solution)/shard_map/ppermute | solution.py:624
  47.6 0.8 copy-start.12
  57.7 17.4 %all-to-all-start.1 = ((bf16[8,256,128]{2,1,0:T(8,128)(2,1)}), bf16[8,256,128]{2,1,0:T(8,128)(2,1)S(1)}, u32[]{:S(2)}, u32[]{:S(2)}) async-start(bf16[8,256,128]{2,1,0:T(8,128)(2,1)} %get-tuple-element.27), calls=%async_computation.1 | async-start | bytes 1048576 | tf_op jit(solution)/shard_map/all_to_all | solution.py:627
  61.4 13.7 %copy-start.2 = (s32[14]{0:T(128)S(1)}, s32[14]{0:T(128)}, u32[]{:S(2)}) copy-start(s32[14]{0:T(128)} %concatenate.3.ids) | copy-start | bytes 172
  68.0 15.8 %copy-start.6 = (bf16[4,512,128]{2,1,0:T(8,128)(2,1)}, bf16[4,512,128]{2,1,0:T(8,128)(2,1)S(1)}, u32[]{:S(2)}) copy-start(bf16[4,512,128]{2,1,0:T(8,128)(2,1)S(1)} %collective-permute-done.6.refs_3_.refs_8_.refs_12_.refs_16_.refs_20_) | copy-start | bytes 1572868
  75.1 9.3 %copy-start = (bf16[8,256,128]{2,1,0:T(8,128)(2,1)}, bf16[8,256,128]{2,1,0:T(8,128)(2,1)S(1)}, u32[]{:S(2)}) copy-start(bf16[8,256,128]{2,1,0:T(8,128)(2,1)S(1)} %all-to-all-done.1.refs_4_.refs_5_) | copy-start | bytes 1572868
  75.1 1.2 copy-start.13
  76.3 0.7 copy-start.16
  77.0 5.8 %copy-start.8 = (bf16[2,128,512]{2,1,0:T(8,128)(2,1)S(1)}, bf16[2,128,512]{2,1,0:T(8,128)(2,1)}, u32[]{:S(2)}) copy-start(bf16[2,128,512]{2,1,0:T(8,128)(2,1)} %get-tuple-element.19.refs_2_.refs_3_) | copy-start | bytes 786436
  77.0 6.3 %copy-start.10 = (bf16[2,128,512]{2,1,0:T(8,128)(2,1)S(1)}, bf16[2,128,512]{2,1,0:T(8,128)(2,1)}, u32[]{:S(2)}) copy-start(bf16[2,128,512]{2,1,0:T(8,128)(2,1)} %copy-done.9) | copy-start | bytes 786436
  78.5 0.6 copy-start.15
  79.1 17.4 %all-to-all-start.2 = ((bf16[8,256,128]{2,1,0:T(8,128)(2,1)}), bf16[8,256,128]{2,1,0:T(8,128)(2,1)S(1)}, u32[]{:S(2)}, u32[]{:S(2)}) async-start(bf16[8,256,128]{2,1,0:T(8,128)(2,1)} %get-tuple-element.28), calls=%async_computation.2 | async-start | bytes 1048576 | tf_op jit(solution)/shard_map/all_to_all | solution.py:627
  82.7 1.6 %collective-permute-start.12 = (bf16[2,128,512]{2,1,0:T(8,128)(2,1)S(1)}, bf16[2,128,512]{2,1,0:T(8,128)(2,1)S(1)}, u32[]{:S(2)}, u32[]{:S(2)}) collective-permute-start(bf16[2,128,512]{2,1,0:T(8,128)(2,1)S(1)} %copy-done.8), channel_id=1, source_target_pairs={{0,1},{1,0},{2,3},{3,2},{4,5},{5,4},{6,7},{7,6},{8,9},{9,8},{10,11... | collective-permute-start | bytes 786440 | tf_op jit(solution)/shard_map/ppermute | solution.py:624
  82.8 3.8 %collective-permute-start.9 = (bf16[8,272,128]{2,1,0:T(8,128)(2,1)S(1)}, bf16[8,272,128]{2,1,0:T(8,128)(2,1)}, u32[]{:S(2)}, u32[]{:S(2)}) collective-permute-start(bf16[8,272,128]{2,1,0:T(8,128)(2,1)S(1)} %copy-done.4), channel_id=1, source_target_pairs={{0,1},{1,0},{2,3},{3,2},{4,5},{5,4},{6,7},{7,6},{8,9},{9,8},{10,11... | collective-permute-start | bytes 1671176 | tf_op jit(solution)/shard_map/ppermute | solution.py:624
  83.3 2.6 %collective-permute-start.10 = (bf16[2,128,512]{2,1,0:T(8,128)(2,1)S(1)}, bf16[2,128,512]{2,1,0:T(8,128)(2,1)S(1)}, u32[]{:S(2)}, u32[]{:S(2)}) collective-permute-start(bf16[2,128,512]{2,1,0:T(8,128)(2,1)S(1)} %copy-done.10), channel_id=1, source_target_pairs={{0,1},{1,0},{2,3},{3,2},{4,5},{5,4},{6,7},{7,6},{8,9},{9,8},{10,11... | collective-permute-start | bytes 786440 | tf_op jit(solution)/shard_map/ppermute | solution.py:624
  83.4 13.1 %collective-permute-start.13 = (bf16[4,512,128]{2,1,0:T(8,128)(2,1)S(1)}, bf16[4,512,128]{2,1,0:T(8,128)(2,1)}, u32[]{:S(2)}, u32[]{:S(2)}) collective-permute-start(bf16[4,512,128]{2,1,0:T(8,128)(2,1)S(1)} %join.1.refs_2_.refs_7_.refs_11_.refs_15_.refs_19_), channel_id=1, source_target_pairs={{0,1},{1,0},{2,3},{3,2},{4,5},{5,4},{6,7},{7,6},{8,9},{9,8},{10,11... | collective-permute-start | bytes 1572872 | tf_op jit(solution)/shard_map/ppermute | solution.py:624
  83.8 12.7 %collective-permute-start.14 = (bf16[4,512,128]{2,1,0:T(8,128)(2,1)S(1)}, bf16[4,512,128]{2,1,0:T(8,128)(2,1)}, u32[]{:S(2)}, u32[]{:S(2)}) collective-permute-start(bf16[4,512,128]{2,1,0:T(8,128)(2,1)S(1)} %collective-permute-done.6.refs_3_.refs_8_.refs_12_.refs_16_.refs_20_), channel_id=1, source_target_pairs={{0,1},{1,0},{2,3},{3,2},{4,5},{5,4},{6,7},{7,6},{8,9},{9,8},{10,11... | collective-permute-start | bytes 1572872 | tf_op jit(solution)/shard_map/ppermute | solution.py:624
  84.3 1.7 %copy-start.20 = (bf16[2,128,512]{2,1,0:T(8,128)(2,1)}, bf16[2,128,512]{2,1,0:T(8,128)(2,1)S(1)}, u32[]{:S(2)}) copy-start(bf16[2,128,512]{2,1,0:T(8,128)(2,1)S(1)} %collective-permute-done.12.refs_6_) | copy-start | bytes 786436
  84.3 12.2 %collective-permute-start.8 = (bf16[8,256,128]{2,1,0:T(8,128)(2,1)S(1)}, bf16[8,256,128]{2,1,0:T(8,128)(2,1)}, u32[]{:S(2)}, u32[]{:S(2)}) collective-permute-start(bf16[8,256,128]{2,1,0:T(8,128)(2,1)S(1)} %all-to-all-done.1.refs_4_.refs_5_), channel_id=1, source_target_pairs={{0,1},{1,0},{2,3},{3,2},{4,5},{5,4},{6,7},{7,6},{8,9},{9,8},{10,11... | collective-permute-start | bytes 1572872 | tf_op jit(solution)/shard_map/ppermute | solution.py:624
  85.9 0.7 copy-start.21
  85.9 10.6 %collective-permute-start.11 = (bf16[2,128,512]{2,1,0:T(8,128)(2,1)S(1)}, bf16[2,128,512]{2,1,0:T(8,128)(2,1)}, u32[]{:S(2)}, u32[]{:S(2)}) collective-permute-start(bf16[2,128,512]{2,1,0:T(8,128)(2,1)S(1)} %collective-permute-done.5.refs_3_.refs_2_), channel_id=1, source_target_pairs={{0,1},{1,0},{2,3},{3,2},{4,5},{5,4},{6,7},{7,6},{8,9},{9,8},{10,11... | collective-permute-start | bytes 786440 | tf_op jit(solution)/shard_map/ppermute | solution.py:624
  96.5 18.8 %copy-start.17 = (bf16[8,256,128]{2,1,0:T(8,128)(2,1)}, bf16[8,256,128]{2,1,0:T(8,128)(2,1)S(1)}, u32[]{:S(2)}) copy-start(bf16[8,256,128]{2,1,0:T(8,128)(2,1)S(1)} %all-to-all-done.2.refs_3_) | copy-start | bytes 1572868
  96.5 18.8 %collective-permute-start.7 = (bf16[8,256,128]{2,1,0:T(8,128)(2,1)S(1)}, bf16[8,256,128]{2,1,0:T(8,128)(2,1)S(1)}, u32[]{:S(2)}, u32[]{:S(2)}) collective-permute-start(bf16[8,256,128]{2,1,0:T(8,128)(2,1)S(1)} %all-to-all-done.2.refs_3_), channel_id=1, source_target_pairs={{0,1},{1,0},{2,3},{3,2},{4,5},{5,4},{6,7},{7,6},{8,9},{9,8},{10,11... | collective-permute-start | bytes 1572872 | tf_op jit(solution)/shard_map/ppermute | solution.py:624
  115.3 0.8 copy-start.19
